TPU v7x, 256 devices: a whole 4x4x8 slice. The times are simulated.
256 devices in a mesh: dp: 8 (over z_lo, y), section: 8 (over z_hi, core), fsdp: 4 (over x).
Axes of the slice: x: 4, y: 4, z: 8 (z_hi: 4, z_lo: 2; z = z_hi * 2 + z_lo), core: 2. Of those that a mesh axis runs over, the one named last changes fastest.
Arguments:
- checkpoints: bfloat16 [8, 2, 4096, 1024], P('section', None, ('dp', 'fsdp')), may hold values from -150 to 150
- cotangent: bfloat16 [2, 4096, 1024], P(None, ('dp', 'fsdp')), may hold values from -6 to 6
- weights: bfloat16 [8, 4, 1024, 1024], P('section', None, ('dp', 'fsdp')), may hold values from -6 to 6
- gains: bfloat16 [8, 1024], P('section', ('dp', 'fsdp')), may hold values from 0.099609375 to 1.8984375
- lengths: int32 [2, 31], replicated, may hold values from 1 to 256, 3840 in all within a row
Outputs:
- frame_grad: bfloat16 [8, 2, 4096, 1024], P('section', None, ('dp', 'fsdp'))
- weight_grad: float32 [8, 4, 1024, 1024], P('section', None, ('dp', 'fsdp'))
- gain_grad: float32 [8, 1024], P('section', ('dp', 'fsdp'))
Inputs may be any that keep to these rules, and one draw needn't show every extreme that they name: Each row of lengths adds up to 3840, and its longest utterance has exactly 256 frames; the last utterance, not listed, has 256 frames.
All inputs are finite; a program needn't handle non-finite values.
Results may differ from a plain program's by a relative error of at most 0.035.
The roundings to bfloat16 on the way count: a program that leaves them out, or rounds other values in their place, can miss the bound.
Values may be sent and summed in bfloat16 or wider, within the bound.
No kernel may reach another device: no remote copies, remote signals or barrier semaphores. Data moves between devices by JAX's collectives and lax.ppermute only.
A program may use at most 128 MiB of HBM per device.

v0:
```python
from functools import partial
import math

import jax
import jax.numpy as jnp
from jax import lax
from jax.sharding import PartitionSpec as P

HEAD = 128
STRETCH = 128


def from_behind(value, axis, steps):
    count = lax.axis_size(axis)
    leading, last = (max(0, -steps), min(count, count - steps))
    return lax.ppermute(value, axis, [(source, source + steps) for source in range(leading, last)])


def normalize(inputs, gain_row):
    as_float = inputs.astype(jnp.float32)
    rscale = lax.rsqrt(jnp.mean(as_float * as_float, axis=-1, keepdims=True) + 1e-06)
    normed = (as_float * rscale * gain_row.astype(jnp.float32)).astype(jnp.bfloat16)
    return (as_float, rscale, normed)


def segment_ids(bounds, places):
    counted = jnp.sum((places[:, None] >= bounds[None, :]).astype(jnp.int32), axis=1)
    return jnp.where(places < 0, -1, counted)


def allowed_rows(block_start, frames, bounds):
    left_span = 2 * STRETCH
    q_index = jnp.arange(frames, dtype=jnp.int32)
    k_index = jnp.arange(left_span + frames, dtype=jnp.int32) - left_span
    q_seg = segment_ids(bounds, block_start + q_index)
    k_seg = segment_ids(bounds, block_start + k_index)
    q_stretch = jnp.floor_divide(q_index, STRETCH)
    k_stretch = jnp.floor_divide(k_index, STRETCH)
    nearby = (k_stretch[None, :] <= q_stretch[:, None]) & (
        k_stretch[None, :] >= q_stretch[:, None] - 2
    )
    return nearby & (q_seg[:, None] == k_seg[None, :])


def project(rows_in, weight):
    full_shape = rows_in.shape
    flat_rows = rows_in.reshape(-1, full_shape[-1])
    return (
        jnp.dot(flat_rows, weight, preferred_element_type=jnp.float32)
        .astype(jnp.bfloat16)
        .reshape(full_shape)
    )


def across(rows_in, weight):
    return lax.dot_general(
        rows_in, weight, (((1,), (1,)), ((), ())), preferred_element_type=jnp.float32
    )


def contract_rows(left_in, right_in):
    return lax.dot_general(
        left_in, right_in, (((0,), (0,)), ((), ())), preferred_element_type=jnp.float32
    )


def attend_block(queries, key_rows, values, allowed, head_count, score_scale):
    micro_count, frames, model_width = queries.shape
    total_keys = key_rows.shape[1]
    query_heads = queries.reshape(micro_count, frames, head_count, HEAD)
    key_heads = key_rows.reshape(micro_count, total_keys, head_count, HEAD)
    value_heads = values.reshape(micro_count, total_keys, head_count, HEAD)
    scores = (
        jnp.einsum("mqhd,mkhd->mhqk", query_heads, key_heads, preferred_element_type=jnp.float32)
        * score_scale
    )
    mask_rows = allowed[:, None, :, :]
    scores = jnp.where(mask_rows, scores, -1e30)
    top_score = jnp.max(scores, axis=-1, keepdims=True)
    expo = jnp.where(mask_rows, jnp.exp(scores - top_score), 0.0)
    soft_probs = expo / jnp.sum(expo, axis=-1, keepdims=True)
    mixed = jnp.einsum(
        "mhqk,mkhd->mqhd",
        soft_probs.astype(jnp.bfloat16),
        value_heads,
        preferred_element_type=jnp.float32,
    )
    return (soft_probs, mixed.reshape(micro_count, frames, model_width).astype(jnp.bfloat16))


def backward_block(
    grad_rows,
    queries,
    key_rows,
    values,
    soft_probs,
    w_query,
    w_key,
    w_value,
    w_out,
    head_count,
    score_scale,
    left_span,
):
    frames, model_width = grad_rows.shape
    total_keys = key_rows.shape[0]
    d_att = across(grad_rows, w_out).astype(jnp.bfloat16)
    att_heads = d_att.reshape(frames, head_count, HEAD)
    value_heads = values.reshape(total_keys, head_count, HEAD)
    key_heads = key_rows.reshape(total_keys, head_count, HEAD)
    query_heads = queries.reshape(frames, head_count, HEAD)
    d_probs = jnp.einsum("qhd,khd->hqk", att_heads, value_heads, preferred_element_type=jnp.float32)
    d_values = jnp.einsum(
        "hqk,qhd->khd",
        soft_probs.astype(jnp.bfloat16),
        att_heads,
        preferred_element_type=jnp.float32,
    )
    d_values = d_values.reshape(total_keys, model_width).astype(jnp.bfloat16)
    d_scores = (
        soft_probs * (d_probs - jnp.sum(d_probs * soft_probs, axis=-1, keepdims=True)) * score_scale
    )
    score_grad = d_scores.astype(jnp.bfloat16)
    d_query = jnp.einsum("hqk,khd->qhd", score_grad, key_heads, preferred_element_type=jnp.float32)
    d_query = d_query.reshape(frames, model_width).astype(jnp.bfloat16)
    d_keys = jnp.einsum("hqk,qhd->khd", score_grad, query_heads, preferred_element_type=jnp.float32)
    d_keys = d_keys.reshape(total_keys, model_width).astype(jnp.bfloat16)
    key_left = d_keys[:left_span]
    key_same = d_keys[left_span:]
    val_left = d_values[:left_span]
    val_same = d_values[left_span:]
    to_left = (across(key_left, w_key) + across(val_left, w_value)).astype(jnp.bfloat16)
    own_part = across(d_query, w_query) + across(key_same, w_key) + across(val_same, w_value)
    return (own_part, to_left, d_query, key_same, val_same, key_left, val_left)


def finish(grad_rows, as_float, rscale, gain_row, d_normed):
    scaled = gain_row.astype(jnp.float32) * d_normed
    cubic = rscale * rscale * rscale
    frame_f = (
        grad_rows.astype(jnp.float32)
        + rscale * scaled
        - as_float * cubic * jnp.mean(scaled * as_float, axis=-1, keepdims=True)
    )
    gain_part = d_normed * as_float * rscale
    return (frame_f, gain_part)


def pick_slot(array_in, slot_index):
    return lax.dynamic_index_in_dim(array_in, slot_index, 0, keepdims=False)


def store_slot(buffer, fresh, slot_index, is_valid):
    current = pick_slot(buffer, slot_index)
    return lax.dynamic_update_index_in_dim(
        buffer, jnp.where(is_valid, fresh, current), slot_index, 0
    )


def body(checkpoints, cotangent, weights, gains, lengths):
    gathered, gain_row = (
        lax.all_gather(weights[0], ("dp", "fsdp"), axis=1, tiled=True),
        lax.all_gather(gains[0], ("dp", "fsdp"), axis=0, tiled=True),
    )
    w_query = gathered[0]
    w_key = gathered[1]
    w_value = gathered[2]
    w_out = gathered[3]
    micro_count, frames, model_width = cotangent.shape
    left_span = 2 * STRETCH
    tail_rows = min(frames, left_span)
    reach_count = left_span // tail_rows
    head_count = model_width // HEAD
    score_scale = 1.0 / math.sqrt(HEAD)
    block_start = lax.axis_index(("dp", "fsdp")) * frames
    as_float, rscale, normed = normalize(checkpoints[0], gain_row)
    left_pieces = []
    for offset in range(reach_count, 0, -1):
        left_pieces.append(from_behind(normed, ("dp", "fsdp"), offset))
    left_rows = jnp.concatenate(left_pieces, axis=1)
    bounds = jnp.cumsum(lengths, axis=1)
    allowed = jax.vmap(partial(allowed_rows, block_start, frames))(bounds)
    key_input = jnp.concatenate([left_rows, normed], axis=1)
    queries = project(normed, w_query)
    key_rows = project(key_input, w_key)
    values = project(key_input, w_value)
    soft_probs, attended = attend_block(queries, key_rows, values, allowed, head_count, score_scale)
    section_count = lax.axis_size("section")
    section_index = lax.axis_index("section")
    zero_rows = jnp.zeros((micro_count, frames, model_width), jnp.bfloat16)
    zero_left = jnp.zeros((micro_count, left_span, model_width), jnp.bfloat16)

    def step(moment, loop_state):
        incoming, outgoing, stored, gain_total = loop_state
        mb_target = moment - (section_count - 1 - section_index)
        is_valid = (mb_target >= 0) & (mb_target < micro_count)
        slot_index = jnp.clip(mb_target, 0, micro_count - 1)
        grad_rows = jnp.where(
            section_index == section_count - 1, pick_slot(cotangent, slot_index), incoming
        )

        def active(grad_block):
            return backward_block(
                grad_block,
                pick_slot(queries, slot_index),
                pick_slot(key_rows, slot_index),
                pick_slot(values, slot_index),
                pick_slot(soft_probs, slot_index),
                w_query,
                w_key,
                w_value,
                w_out,
                head_count,
                score_scale,
                left_span,
            )

        def resting(grad_block):
            rows_zero = jnp.zeros((frames, model_width), jnp.bfloat16)
            left_zero = jnp.zeros((left_span, model_width), jnp.bfloat16)
            return (
                jnp.zeros((frames, model_width), jnp.float32),
                left_zero,
                rows_zero,
                rows_zero,
                rows_zero,
                left_zero,
                left_zero,
            )

        own_part, to_left, d_query, key_same, val_same, key_left, val_left = lax.cond(
            is_valid, active, resting, grad_rows
        )
        received = jnp.zeros((tail_rows, model_width), jnp.float32)
        for offset in range(1, reach_count + 1):
            left_part = to_left[
                (reach_count - offset) * tail_rows : (reach_count - offset + 1) * tail_rows
            ]
            received = received + from_behind(left_part, ("dp", "fsdp"), -offset).astype(
                jnp.float32
            )
        d_normed = own_part.at[frames - tail_rows :].add(received)
        frame_f, gain_part = finish(
            grad_rows,
            pick_slot(as_float, slot_index),
            pick_slot(rscale, slot_index),
            gain_row,
            d_normed,
        )
        frame_out = frame_f.astype(jnp.bfloat16)
        outgoing = store_slot(outgoing, frame_out, slot_index, is_valid)
        fresh_rows = (grad_rows, d_query, key_same, val_same, key_left, val_left)
        stored = tuple(
            (
                store_slot(buffer, fresh, slot_index, is_valid)
                for buffer, fresh in zip(stored, fresh_rows)
            )
        )
        gain_total = gain_total + jnp.where(is_valid, jnp.sum(gain_part, axis=0), 0.0)
        incoming = from_behind(frame_out, "section", -1)
        return (incoming, outgoing, stored, gain_total)

    start_state = (
        jnp.zeros((frames, model_width), jnp.bfloat16),
        zero_rows,
        (zero_rows, zero_rows, zero_rows, zero_rows, zero_left, zero_left),
        jnp.zeros((model_width,), jnp.float32),
    )
    incoming, outgoing, stored, gain_total = lax.fori_loop(
        0, section_count + micro_count - 1, step, start_state
    )
    grad_rows, d_query, key_same, val_same, key_left, val_left = stored
    flat_normed = normed.reshape(-1, model_width)
    flat_left = left_rows.reshape(-1, model_width)
    flat_att = attended.reshape(-1, model_width)
    flat_grad = grad_rows.reshape(-1, model_width)
    flat_dq = d_query.reshape(-1, model_width)
    flat_ks = key_same.reshape(-1, model_width)
    flat_vs = val_same.reshape(-1, model_width)
    flat_kl = key_left.reshape(-1, model_width)
    flat_vl = val_left.reshape(-1, model_width)
    term = jnp.stack(
        [
            contract_rows(flat_normed, flat_dq),
            contract_rows(flat_normed, flat_ks) + contract_rows(flat_left, flat_kl),
            contract_rows(flat_normed, flat_vs) + contract_rows(flat_left, flat_vl),
            contract_rows(flat_att, flat_grad),
        ]
    )
    weight_part, gain_sum = (
        lax.psum_scatter(
            term.astype(jnp.bfloat16), ("dp", "fsdp"), scatter_dimension=1, tiled=True
        ).astype(jnp.float32),
        lax.psum_scatter(
            gain_total.astype(jnp.bfloat16), ("dp", "fsdp"), scatter_dimension=0, tiled=True
        ).astype(jnp.float32),
    )
    return (outgoing[None], weight_part[None], gain_sum[None])


def solution(mesh):
    placed = (
        P("section", None, ("dp", "fsdp"), None),
        P(None, ("dp", "fsdp"), None),
        P("section", None, ("dp", "fsdp"), None),
        P("section", ("dp", "fsdp")),
        P(),
    )
    return jax.shard_map(
        body,
        mesh=mesh,
        in_specs=placed,
        out_specs=(
            P("section", None, ("dp", "fsdp"), None),
            P("section", None, ("dp", "fsdp"), None),
            P("section", ("dp", "fsdp")),
        ),
        check_vma=False,
    )
```

profile of v0, /device:TPU:32, one launch (start us, length us, event | category | flops | bytes accessed | tf_op | source)
XLA Modules:
  0.0 1147.3 jit_solution(16708265724235754876)
XLA Ops:
  10.9 81.9 %all-reduce = bf16[1024]{0:T(1024)(128)(2,1)S(1)} all-reduce(bf16[1024]{0:T(1024)(128)(2,1)S(1)} %dynamic-update-slice.2), channel_id=2, replica_groups=mesh['dp'=8,'section'=8,'fsdp'=4] {'dp','fsdp'}, use_global_device_ids=true, to_apply=%add | all-reduce | flops 1024 | bytes 4096 | tf_op jit(solution)/shard_map/all_gather | solution.py:163
  101.6 13.3 %collective-permute-done.3 = bf16[2,128,1024]{1,2,0:T(8,128)(2,1)S(1)} collective-permute-done((bf16[2,128,1024]{1,2,0:T(8,128)(2,1)S(1)}, bf16[2,128,1024]{1,2,0:T(8,128)(2,1)S(1)}, u32[]{:S(2)}, u32[]{:S(2)}) %collective-permute-start.3) | collective-permute-done | bytes 524320 | tf_op jit(solution)/shard_map/ppermute | solution.py:16
  114.9 26.6 %collective-permute-done.4 = bf16[2,128,1024]{1,2,0:T(8,128)(2,1)S(1)} collective-permute-done((bf16[2,128,1024]{1,2,0:T(8,128)(2,1)S(1)}, bf16[2,128,1024]{1,2,0:T(8,128)(2,1)S(1)}, u32[]{:S(2)}, u32[]{:S(2)}) %collective-permute-start.4) | collective-permute-done | bytes 524320 | tf_op jit(solution)/shard_map/ppermute | solution.py:16
  145.0 45.2 %all-gather.4.cloned.1.call-done = bf16[1,4,1024,1024]{3,2,1,0:T(8,128)(2,1)} async-done(((bf16[1,4,32,1024]{3,2,1,0:T(8,128)(2,1)}), bf16[1,4,1024,1024]{3,2,1,0:T(8,128)(2,1)}) %all-gather.4.cloned.1.call-update) | async-done | bytes 8388624 | tf_op jit(solution)/shard_map/all_gather | solution.py:162
  220.3 720.9 %while.40 = (s32[]{:T(128)}, bf16[128,1024]{0,1:T(8,128)(2,1)}, bf16[2,128,1024]{2,1,0:T(8,128)(2,1)}, bf16[2,128,1024]{1,2,0:T(8,128)(2,1)}, bf16[2,128,1024]{1...) while((s32[]{:T(128)}, bf16[128,1024]{0,1:T(8,128)(2,1)}, ...), condition=%wide.region_12.13_spmd.clone, body=%wide.region_6.12_spmd.clone.sunk | while | flops 2560104448 | bytes 129016488 | solution.py:269
  225.7 5.6 conditional.3
  271.0 5.6 conditional.3
  304.2 9.2 collective-permute-done.2
  353.0 9.3 collective-permute-done.2
  379.9 5.8 collective-permute-start.1
  405.6 6.3 collective-permute-done.2
  427.6 6.5 collective-permute-start
  457.3 6.2 collective-permute-done.2
  469.7 5.6 conditional.3
  479.2 7.0 collective-permute-start
  486.3 5.7 collective-permute-start.1
  511.8 6.3 collective-permute-done.2
  524.2 5.6 conditional.3
  558.8 218.4 %collective-permute-done.2 = bf16[128,1024]{0,1:T(8,128)(2,1)S(1)} collective-permute-done((bf16[128,1024]{0,1:T(8,128)(2,1)}, bf16[128,1024]{0,1:T(8,128)(2,1)S(1)}, u32[]{:S(2)}, u32[]{:S(2)}) %collective-permute-start.2) | collective-permute-done | bytes 262176 | tf_op jit(solution)/shard_map/while/body/eval_jaxpr/ppermute | solution.py:16
  783.3 38.9 %conditional.3 = (bf16[256,1024]{1,0:T(8,128)(2,1)}, bf16[128,1024]{0,1:T(8,128)(2,1)}, bf16[128,1024]{0,1:T(8,128)(2,1)}, bf16[128,1024]{0,1:T(8,128)(2,1)}, bf...) conditional(s32[]{:T(128)} %convert_element_type.244, () %tuple.114, (s32[]{:T(128)}, ...), branch_computations={%region_7.7_spmd, %region_8.9_spmd} | conditional | flops 2555906816 | bytes 82315552 | solution.py:231
  852.8 10.4 collective-permute-done.2
  869.3 38.9 %conditional.3 = (bf16[256,1024]{1,0:T(8,128)(2,1)}, bf16[128,1024]{0,1:T(8,128)(2,1)}, bf16[128,1024]{0,1:T(8,128)(2,1)}, bf16[128,1024]{0,1:T(8,128)(2,1)}, bf...) conditional(s32[]{:T(128)} %convert_element_type.244, () %tuple.114, (s32[]{:T(128)}, ...), branch_computations={%region_7.7_spmd, %region_8.9_spmd} | conditional | flops 2555906816 | bytes 82315552 | solution.py:231
  957.7 78.4 %all-reduce.1 = bf16[1024]{0:T(1024)(128)(2,1)S(1)} all-reduce(bf16[1024]{0:T(1024)(128)(2,1)S(1)} %convert_element_type.164), channel_id=5, replica_groups=mesh['dp'=8,'section'=8,'fsdp'=4] {'dp','fsdp'}, use_global_device_ids=true, to_apply=%region_14.15.clone | all-reduce | flops 1024 | bytes 4096
  1036.7 102.0 %reduce-scatter.2.cloned.1.call-done = bf16[4,32,1024]{2,1,0:T(8,128)(2,1)} async-done(((bf16[4,1024,1024]{2,1,0:T(8,128)(2,1)}), bf16[4,32,1024]{2,1,0:T(8,128)(2,1)}) %reduce-scatter.2.cloned.1.call-update) | async-done | bytes 262160 | tf_op jit(solution)/shard_map/reduce_scatter | solution.py:291
  (694 shorter events, 508.0 us)
Async XLA Ops:
  7.2 183.1 %all-gather.4.cloned.1.call-start = ((), (), s32[]{:S(2)}) async-start(), calls=%async_computation.2 | async-start | bytes 8650752 | tf_op jit(solution)/shard_map/all_gather | solution.py:162
  7.9 1130.7 %reduce-scatter.2.cloned.1.call-start = ((), (), s32[]{:S(2)}) async-start(), calls=%async_computation.1 | async-start | bytes 8650752 | tf_op jit(solution)/shard_map/reduce_scatter | solution.py:291
  94.5 20.4 %collective-permute-start.3 = (bf16[2,128,1024]{1,2,0:T(8,128)(2,1)S(1)}, bf16[2,128,1024]{1,2,0:T(8,128)(2,1)S(1)}, u32[]{:S(2)}, u32[]{:S(2)}) collective-permute-start(bf16[2,128,1024]{1,2,0:T(8,128)(2,1)S(1)} %multiply_convert_fusion), channel_id=1, source_target_pairs={{0,2},{1,3},{2,32},{3,33},{32,34},{33,35},{34,64},{35,65},{64,66},... | collective-permute-start | bytes 1572872 | tf_op jit(solution)/shard_map/ppermute | solution.py:16
  96.5 45.0 %collective-permute-start.4 = (bf16[2,128,1024]{1,2,0:T(8,128)(2,1)S(1)}, bf16[2,128,1024]{1,2,0:T(8,128)(2,1)S(1)}, u32[]{:S(2)}, u32[]{:S(2)}) collective-permute-start(bf16[2,128,1024]{1,2,0:T(8,128)(2,1)S(1)} %multiply_convert_fusion), channel_id=1, source_target_pairs={{0,1},{1,2},{2,3},{3,32},{32,33},{33,34},{34,35},{35,64},{64,65},{... | collective-permute-start | bytes 1572872 | tf_op jit(solution)/shard_map/ppermute | solution.py:16
  235.3 20.6 %collective-permute-start = (bf16[128,1024]{0,1:T(8,128)(2,1)}, bf16[128,1024]{0,1:T(8,128)(2,1)}, u32[]{:S(2)}, u32[]{:S(2)}) collective-permute-start(bf16[128,1024]{0,1:T(8,128)(2,1)} %get-tuple-element.1091), channel_id=1, source_target_pairs={{2,0},{3,1},{32,2},{33,3},{34,32},{35,33},{64,34},{65,35},{66,64},... | collective-permute-start | bytes 786440 | tf_op jit(solution)/shard_map/while/body/eval_jaxpr/ppermute | solution.py:16
  240.2 15.6 %collective-permute-start.1 = (bf16[128,1024]{0,1:T(8,128)(2,1)}, bf16[128,1024]{0,1:T(8,128)(2,1)}, u32[]{:S(2)}, u32[]{:S(2)}) collective-permute-start(bf16[128,1024]{0,1:T(8,128)(2,1)} %get-tuple-element.1092), channel_id=1, source_target_pairs={{1,0},{2,1},{3,2},{32,3},{33,32},{34,33},{35,34},{64,35},{65,64},{... | collective-permute-start | bytes 786440 | tf_op jit(solution)/shard_map/while/body/eval_jaxpr/ppermute | solution.py:16
  280.6 16.3 %collective-permute-start = (bf16[128,1024]{0,1:T(8,128)(2,1)}, bf16[128,1024]{0,1:T(8,128)(2,1)}, u32[]{:S(2)}, u32[]{:S(2)}) collective-permute-start(bf16[128,1024]{0,1:T(8,128)(2,1)} %get-tuple-element.1091), channel_id=1, source_target_pairs={{2,0},{3,1},{32,2},{33,3},{34,32},{35,33},{64,34},{65,35},{66,64},... | collective-permute-start | bytes 786440 | tf_op jit(solution)/shard_map/while/body/eval_jaxpr/ppermute | solution.py:16
  282.5 14.4 %collective-permute-start.1 = (bf16[128,1024]{0,1:T(8,128)(2,1)}, bf16[128,1024]{0,1:T(8,128)(2,1)}, u32[]{:S(2)}, u32[]{:S(2)}) collective-permute-start(bf16[128,1024]{0,1:T(8,128)(2,1)} %get-tuple-element.1092), channel_id=1, source_target_pairs={{1,0},{2,1},{3,2},{32,3},{33,32},{34,33},{35,34},{64,35},{65,64},{... | collective-permute-start | bytes 786440 | tf_op jit(solution)/shard_map/while/body/eval_jaxpr/ppermute | solution.py:16
  329.1 16.5 %collective-permute-start = (bf16[128,1024]{0,1:T(8,128)(2,1)}, bf16[128,1024]{0,1:T(8,128)(2,1)}, u32[]{:S(2)}, u32[]{:S(2)}) collective-permute-start(bf16[128,1024]{0,1:T(8,128)(2,1)} %get-tuple-element.1091), channel_id=1, source_target_pairs={{2,0},{3,1},{32,2},{33,3},{34,32},{35,33},{64,34},{65,35},{66,64},... | collective-permute-start | bytes 786440 | tf_op jit(solution)/shard_map/while/body/eval_jaxpr/ppermute | solution.py:16
  331.0 14.6 %collective-permute-start.1 = (bf16[128,1024]{0,1:T(8,128)(2,1)}, bf16[128,1024]{0,1:T(8,128)(2,1)}, u32[]{:S(2)}, u32[]{:S(2)}) collective-permute-start(bf16[128,1024]{0,1:T(8,128)(2,1)} %get-tuple-element.1092), channel_id=1, source_target_pairs={{1,0},{2,1},{3,2},{32,3},{33,32},{34,33},{35,34},{64,35},{65,64},{... | collective-permute-start | bytes 786440 | tf_op jit(solution)/shard_map/while/body/eval_jaxpr/ppermute | solution.py:16
  378.0 20.2 %collective-permute-start = (bf16[128,1024]{0,1:T(8,128)(2,1)}, bf16[128,1024]{0,1:T(8,128)(2,1)}, u32[]{:S(2)}, u32[]{:S(2)}) collective-permute-start(bf16[128,1024]{0,1:T(8,128)(2,1)} %get-tuple-element.1091), channel_id=1, source_target_pairs={{2,0},{3,1},{32,2},{33,3},{34,32},{35,33},{64,34},{65,35},{66,64},... | collective-permute-start | bytes 786440 | tf_op jit(solution)/shard_map/while/body/eval_jaxpr/ppermute | solution.py:16
  379.9 18.3 %collective-permute-start.1 = (bf16[128,1024]{0,1:T(8,128)(2,1)}, bf16[128,1024]{0,1:T(8,128)(2,1)}, u32[]{:S(2)}, u32[]{:S(2)}) collective-permute-start(bf16[128,1024]{0,1:T(8,128)(2,1)} %get-tuple-element.1092), channel_id=1, source_target_pairs={{1,0},{2,1},{3,2},{32,3},{33,32},{34,33},{35,34},{64,35},{65,64},{... | collective-permute-start | bytes 786440 | tf_op jit(solution)/shard_map/while/body/eval_jaxpr/ppermute | solution.py:16
  427.6 22.4 %collective-permute-start = (bf16[128,1024]{0,1:T(8,128)(2,1)}, bf16[128,1024]{0,1:T(8,128)(2,1)}, u32[]{:S(2)}, u32[]{:S(2)}) collective-permute-start(bf16[128,1024]{0,1:T(8,128)(2,1)} %get-tuple-element.1091), channel_id=1, source_target_pairs={{2,0},{3,1},{32,2},{33,3},{34,32},{35,33},{64,34},{65,35},{66,64},... | collective-permute-start | bytes 786440 | tf_op jit(solution)/shard_map/while/body/eval_jaxpr/ppermute | solution.py:16
  434.1 15.8 %collective-permute-start.1 = (bf16[128,1024]{0,1:T(8,128)(2,1)}, bf16[128,1024]{0,1:T(8,128)(2,1)}, u32[]{:S(2)}, u32[]{:S(2)}) collective-permute-start(bf16[128,1024]{0,1:T(8,128)(2,1)} %get-tuple-element.1092), channel_id=1, source_target_pairs={{1,0},{2,1},{3,2},{32,3},{33,32},{34,33},{35,34},{64,35},{65,64},{... | collective-permute-start | bytes 786440 | tf_op jit(solution)/shard_map/while/body/eval_jaxpr/ppermute | solution.py:16
  479.2 25.1 %collective-permute-start = (bf16[128,1024]{0,1:T(8,128)(2,1)}, bf16[128,1024]{0,1:T(8,128)(2,1)}, u32[]{:S(2)}, u32[]{:S(2)}) collective-permute-start(bf16[128,1024]{0,1:T(8,128)(2,1)} %get-tuple-element.1091), channel_id=1, source_target_pairs={{2,0},{3,1},{32,2},{33,3},{34,32},{35,33},{64,34},{65,35},{66,64},... | collective-permute-start | bytes 786440 | tf_op jit(solution)/shard_map/while/body/eval_jaxpr/ppermute | solution.py:16
  486.3 18.1 %collective-permute-start.1 = (bf16[128,1024]{0,1:T(8,128)(2,1)}, bf16[128,1024]{0,1:T(8,128)(2,1)}, u32[]{:S(2)}, u32[]{:S(2)}) collective-permute-start(bf16[128,1024]{0,1:T(8,128)(2,1)} %get-tuple-element.1092), channel_id=1, source_target_pairs={{1,0},{2,1},{3,2},{32,3},{33,32},{34,33},{35,34},{64,35},{65,64},{... | collective-permute-start | bytes 786440 | tf_op jit(solution)/shard_map/while/body/eval_jaxpr/ppermute | solution.py:16
  533.7 17.7 %collective-permute-start = (bf16[128,1024]{0,1:T(8,128)(2,1)}, bf16[128,1024]{0,1:T(8,128)(2,1)}, u32[]{:S(2)}, u32[]{:S(2)}) collective-permute-start(bf16[128,1024]{0,1:T(8,128)(2,1)} %get-tuple-element.1091), channel_id=1, source_target_pairs={{2,0},{3,1},{32,2},{33,3},{34,32},{35,33},{64,34},{65,35},{66,64},... | collective-permute-start | bytes 786440 | tf_op jit(solution)/shard_map/while/body/eval_jaxpr/ppermute | solution.py:16
  535.9 15.5 %collective-permute-start.1 = (bf16[128,1024]{0,1:T(8,128)(2,1)}, bf16[128,1024]{0,1:T(8,128)(2,1)}, u32[]{:S(2)}, u32[]{:S(2)}) collective-permute-start(bf16[128,1024]{0,1:T(8,128)(2,1)} %get-tuple-element.1092), channel_id=1, source_target_pairs={{1,0},{2,1},{3,2},{32,3},{33,32},{34,33},{35,34},{64,35},{65,64},{... | collective-permute-start | bytes 786440 | tf_op jit(solution)/shard_map/while/body/eval_jaxpr/ppermute | solution.py:16
  556.8 220.4 %collective-permute-start.2 = (bf16[128,1024]{0,1:T(8,128)(2,1)}, bf16[128,1024]{0,1:T(8,128)(2,1)S(1)}, u32[]{:S(2)}, u32[]{:S(2)}) collective-permute-start(bf16[128,1024]{0,1:T(8,128)(2,1)} %get-tuple-element.1095), channel_id=1, source_target_pairs={{4,0},{8,4},{12,8},{16,12},{20,16},{24,20},{28,24},{5,1},{9,5},{13... | collective-permute-start | bytes 786440 | tf_op jit(solution)/shard_map/while/body/eval_jaxpr/ppermute | solution.py:16
  826.2 19.2 %collective-permute-start = (bf16[128,1024]{0,1:T(8,128)(2,1)}, bf16[128,1024]{0,1:T(8,128)(2,1)}, u32[]{:S(2)}, u32[]{:S(2)}) collective-permute-start(bf16[128,1024]{0,1:T(8,128)(2,1)} %get-tuple-element.1091), channel_id=1, source_target_pairs={{2,0},{3,1},{32,2},{33,3},{34,32},{35,33},{64,34},{65,35},{66,64},... | collective-permute-start | bytes 786440 | tf_op jit(solution)/shard_map/while/body/eval_jaxpr/ppermute | solution.py:16
  828.1 17.3 %collective-permute-start.1 = (bf16[128,1024]{0,1:T(8,128)(2,1)}, bf16[128,1024]{0,1:T(8,128)(2,1)}, u32[]{:S(2)}, u32[]{:S(2)}) collective-permute-start(bf16[128,1024]{0,1:T(8,128)(2,1)} %get-tuple-element.1092), channel_id=1, source_target_pairs={{1,0},{2,1},{3,2},{32,3},{33,32},{34,33},{35,34},{64,35},{65,64},{... | collective-permute-start | bytes 786440 | tf_op jit(solution)/shard_map/while/body/eval_jaxpr/ppermute | solution.py:16
  850.8 12.4 %collective-permute-start.2 = (bf16[128,1024]{0,1:T(8,128)(2,1)}, bf16[128,1024]{0,1:T(8,128)(2,1)S(1)}, u32[]{:S(2)}, u32[]{:S(2)}) collective-permute-start(bf16[128,1024]{0,1:T(8,128)(2,1)} %get-tuple-element.1095), channel_id=1, source_target_pairs={{4,0},{8,4},{12,8},{16,12},{20,16},{24,20},{28,24},{5,1},{9,5},{13... | collective-permute-start | bytes 786440 | tf_op jit(solution)/shard_map/while/body/eval_jaxpr/ppermute | solution.py:16
  912.2 19.3 %collective-permute-start = (bf16[128,1024]{0,1:T(8,128)(2,1)}, bf16[128,1024]{0,1:T(8,128)(2,1)}, u32[]{:S(2)}, u32[]{:S(2)}) collective-permute-start(bf16[128,1024]{0,1:T(8,128)(2,1)} %get-tuple-element.1091), channel_id=1, source_target_pairs={{2,0},{3,1},{32,2},{33,3},{34,32},{35,33},{64,34},{65,35},{66,64},... | collective-permute-start | bytes 786440 | tf_op jit(solution)/shard_map/while/body/eval_jaxpr/ppermute | solution.py:16
  914.1 17.4 %collective-permute-start.1 = (bf16[128,1024]{0,1:T(8,128)(2,1)}, bf16[128,1024]{0,1:T(8,128)(2,1)}, u32[]{:S(2)}, u32[]{:S(2)}) collective-permute-start(bf16[128,1024]{0,1:T(8,128)(2,1)} %get-tuple-element.1092), channel_id=1, source_target_pairs={{1,0},{2,1},{3,2},{32,3},{33,32},{34,33},{35,34},{64,35},{65,64},{... | collective-permute-start | bytes 786440 | tf_op jit(solution)/shard_map/while/body/eval_jaxpr/ppermute | solution.py:16
  (146 other events, 705.8 us)
Sparse Core Ops, SparseCore 0:
  9.8 180.4 all-gather.3
  957.1 181.4 reduce-scatter.1
where the time goes:
time: 1150 us
  waiting for transfers between devices  457 us (40%)
  local copies, waits for them, and re-layouts  264 us (23%)
  blocking collectives  160 us (14%)
  other arithmetic  102 us (9%)
  starting transfers between devices  76.1 us (7%)
  matrix products  69.5 us (6%)
  between operations  15.7 us (1%)
    ppermute x29, waiting for transfers between devices, from_behind(): lax.ppermute(value, axis, [(source, source + steps) for source in range(l...  309 us
    dynamic_slice x94, local copies, waits for them, and re-layouts, pick_slot(): return lax.dynamic_index_in_dim(array_in, slot_index, 0, keepdims=False)  118 us
    reduce_scatter x1, waiting for transfers between devices, body(): lax.psum_scatter(term.astype(jnp.bfloat16), ('dp', 'fsdp'), scatter_dimen...  102 us
    all_gather x1, blocking collectives, body(): lax.all_gather(gains[0], ('dp', 'fsdp'), axis=0, tiled=True)  81.9 us
    unnamed x1, blocking collectives  78.4 us
    ppermute x29, starting transfers between devices, from_behind(): lax.ppermute(value, axis, [(source, source + steps) for source in range(l...  76 us
    dynamic_update_slice x36, other arithmetic, store_slot(): lax.dynamic_update_index_in_dim(buffer, jnp.where(is_valid, fresh, curren...  53.4 us
    all_gather x1, waiting for transfers between devices, body(): lax.all_gather(weights[0], ('dp', 'fsdp'), axis=1, tiled=True)  45.2 us
  transfers between devices with their start and end apart: 31, of which 13 were waited for; matrix products, arithmetic and copies ran while one was open for 12% of the time, Pallas kernels for 0%

commit v1 on v0

v1 whole, which is shorter than its diff:
```python
from functools import partial
import math

import jax
import jax.numpy as jnp
from jax import lax
from jax.experimental import pallas as pl
from jax.experimental.pallas import tpu as pltpu
from jax.sharding import PartitionSpec as P

HEAD = 128
BLOCK = 128
WIDTH = 1024
HEADS = WIDTH // HEAD
MICRO = 2
SCALE = 1.0 / math.sqrt(HEAD)
GROUP = ("dp", "fsdp")
EVERY = ("dp", "section", "fsdp")
VMEM_LIMIT = 52 * 1024 * 1024


def dot(left, right):
    return lax.dot_general(left, right, (((1,), (0,)), ((), ())), preferred_element_type=jnp.float32)


def dot_nt(left, right):
    return lax.dot_general(left, right, (((1,), (1,)), ((), ())), preferred_element_type=jnp.float32)


def dot_tn(left, right):
    return lax.dot_general(left, right, (((0,), (0,)), ((), ())), preferred_element_type=jnp.float32)


def shift(value, steps):
    count = lax.axis_size(GROUP)
    pairs = [(b, b + steps) for b in range(count) if 0 <= b + steps < count]
    return lax.ppermute(value, GROUP, pairs)


def hop(value, source, target, back):
    sections, rows = lax.axis_size("section"), lax.axis_size("fsdp")
    count = lax.axis_size(GROUP)

    def place(section, block):
        return (block // rows * sections + section) * rows + block % rows

    pairs = [(place(source, b), place(target, b - back)) for b in range(back, count)]
    return lax.ppermute(value, EVERY, pairs)


def group_dims():
    dp, fsdp = lax.axis_size("dp"), lax.axis_size("fsdp")
    planes = 2 if dp % 2 == 0 else 1
    return (planes, dp // planes, fsdp)


def turn(value, axis, steps):
    dims = group_dims()
    pairs = []
    for z in range(dims[0]):
        for y in range(dims[1]):
            for x in range(dims[2]):
                at = [z, y, x]
                to = list(at)
                to[axis] = (at[axis] + steps) % dims[axis]
                index = lambda p: (p[0] * dims[1] + p[1]) * dims[2] + p[2]
                pairs.append((index(at), index(to)))
    return lax.ppermute(value, GROUP, pairs)


def group_sum(value):
    for axis, size in enumerate(group_dims()):
        value = sum([turn(value, axis, steps) for steps in range(1, size)], value)
    return value


def normed(x, gain):
    as_float = x.astype(jnp.float32)
    rscale = lax.rsqrt(jnp.mean(as_float * as_float, axis=-1, keepdims=True) + 1e-06)
    return (as_float * rscale * gain).astype(jnp.bfloat16)


def forward_kernel(
    l2, l1, own, r1, r2, w, gain, seg_col, seg_row,
    h_out, q_out, k_out, v_out, p_out, pt_out, o_out, a_out,
    h5, q3, k5, v5,
):
    gain_row = gain[0:1, :]
    for at, part in enumerate((l2, l1, own, r1, r2)):
        h5[at * BLOCK : (at + 1) * BLOCK, :] = normed(part[0], gain_row)
    h_out[0] = h5[2 * BLOCK : 3 * BLOCK, :]
    for n in range(0, WIDTH, 256):
        cols = slice(n, n + 256)
        q3[:, cols] = dot(h5[2 * BLOCK :, :], w[0, :, cols]).astype(jnp.bfloat16)
        k5[:, cols] = dot(h5[...], w[1, :, cols]).astype(jnp.bfloat16)
        v5[:, cols] = dot(h5[...], w[2, :, cols]).astype(jnp.bfloat16)
    q_out[0] = q3[...]
    k_out[0] = k5[: 3 * BLOCK, :]
    v_out[0] = v5[: 3 * BLOCK, :]
    for head in range(HEADS):
        cols = slice(head * HEAD, (head + 1) * HEAD)
        for j in range(3):
            rows = slice(j * BLOCK, (j + 1) * BLOCK)
            keys = slice(j * BLOCK, (j + 3) * BLOCK)
            allowed = seg_col[0, (j + 2) * BLOCK : (j + 3) * BLOCK, 0:1] == seg_row[0, 0:1, keys]
            score = jnp.where(allowed, dot_nt(q3[rows, cols], k5[keys, cols]) * SCALE, -1e30)
            top = jnp.max(score, axis=-1, keepdims=True)
            expo = jnp.where(allowed, jnp.exp(score - top), 0.0)
            p = expo / jnp.sum(expo, axis=-1, keepdims=True)
            high = p.astype(jnp.bfloat16)
            low = (p - high.astype(jnp.float32)).astype(jnp.bfloat16)
            values = v5[keys, cols]
            mixed = dot(high, values)
            o_out[0, rows, cols] = mixed + dot(low, values)
            if j == 0:
                p_out[0, head] = p
                a_out[0, :, cols] = mixed.astype(jnp.bfloat16)
            pt_out[0, head, :, rows] = p[:, (2 - j) * BLOCK : (3 - j) * BLOCK].T


def forward(parts, w, gain, seg_col, seg_row):
    def per_micro(shape):
        return pl.BlockSpec((1,) + shape, lambda m: (m,) + (0,) * len(shape))

    def whole(shape):
        return pl.BlockSpec(shape, lambda m: (0,) * len(shape), pipeline_mode=pl.Buffered(1))

    outs = [
        ((BLOCK, WIDTH), jnp.bfloat16),
        ((3 * BLOCK, WIDTH), jnp.bfloat16),
        ((3 * BLOCK, WIDTH), jnp.bfloat16),
        ((3 * BLOCK, WIDTH), jnp.bfloat16),
        ((HEADS, BLOCK, 3 * BLOCK), jnp.float32),
        ((HEADS, BLOCK, 3 * BLOCK), jnp.float32),
        ((3 * BLOCK, WIDTH), jnp.float32),
        ((BLOCK, WIDTH), jnp.bfloat16),
    ]
    return pl.pallas_call(
        forward_kernel,
        grid=(MICRO,),
        in_specs=[per_micro((BLOCK, WIDTH))] * 5
        + [
            whole((3, WIDTH, WIDTH)),
            whole((8, WIDTH)),
            per_micro((5 * BLOCK, 1)),
            per_micro((1, 5 * BLOCK)),
        ],
        out_specs=[per_micro(shape) for shape, _ in outs],
        out_shape=[jax.ShapeDtypeStruct((MICRO,) + shape, kind) for shape, kind in outs],
        scratch_shapes=[
            pltpu.VMEM((5 * BLOCK, WIDTH), jnp.bfloat16),
            pltpu.VMEM((3 * BLOCK, WIDTH), jnp.bfloat16),
            pltpu.VMEM((5 * BLOCK, WIDTH), jnp.bfloat16),
            pltpu.VMEM((5 * BLOCK, WIDTH), jnp.bfloat16),
        ],
        compiler_params=pltpu.CompilerParams(vmem_limit_bytes=VMEM_LIMIT),
        cost_estimate=pl.CostEstimate(
            flops=2 * 2 * 15 * BLOCK * WIDTH * WIDTH, bytes_accessed=28 << 20, transcendentals=0
        ),
        name="forward",
    )(*parts, w, gain, seg_col, seg_row)


def backward_kernel(micro, first, *refs):
    flag, g0, g1, g2, w, q_in, k_in, v_in, p_in, pt_in, o_in, x_in, gain_in = refs[:13]
    refs = refs[13 if first else 19 :]
    frame_out, g_out, dq_out, dk_out, dv_out, gain_out = refs[:6]
    g, wv, q, k, v, p, pt, o, x, gain, da, dq, dk, dv, dh, frame, gain_sum, sems = refs[6:]

    @pl.when(flag[0] == 1)
    def _():
        def move(at, source, target):
            copy = pltpu.make_async_copy(source, target, sems.at[at])
            copy.start()
            return copy

        load_g = [
            move(at, part, g.at[pl.ds(at * BLOCK, BLOCK), :]) for at, part in enumerate((g0, g1, g2))
        ]
        load_wo = move(3, w.at[3], wv.at[3])
        load_o = move(4, o_in.at[micro], o)
        load_v = move(5, v_in.at[micro], v)
        load_p = move(6, p_in.at[micro], p)
        load_k = move(7, k_in.at[micro], k)
        load_pt = move(8, pt_in.at[micro], pt)
        load_q = move(9, q_in.at[micro], q)
        load_w = move(10, w.at[pl.ds(0, 3)], wv.at[pl.ds(0, 3)])
        load_x = move(11, x_in.at[micro], x)
        load_gain = move(12, gain_in, gain)
        for copy in load_g:
            copy.wait()
        load_wo.wait()
        store_g = move(13, g.at[pl.ds(0, BLOCK), :], g_out)
        for n in range(0, WIDTH, 256):
            cols = slice(n, n + 256)
            da[:, cols] = dot_nt(g[...], wv[3, cols, :]).astype(jnp.bfloat16)
        for copy in (load_o, load_v, load_p, load_k, load_pt, load_q):
            copy.wait()
        for head in range(HEADS):
            cols = slice(head * HEAD, (head + 1) * HEAD)
            da_h = da[:, cols]
            inner = jnp.sum(da_h.astype(jnp.float32) * o[:, cols], axis=-1, keepdims=True)
            dp = dot_nt(da_h[:BLOCK], v[:, cols])
            ds = (p[head] * (dp - inner[:BLOCK]) * SCALE).astype(jnp.bfloat16)
            dq[:, cols] = dot(ds, k[:, cols]).astype(jnp.bfloat16)
            inner_row = jnp.broadcast_to(inner, (3 * BLOCK, HEAD)).T
            p_t = pt[head]
            dp_t = dot_nt(v[2 * BLOCK :, cols], da_h)
            ds_t = (p_t * (dp_t - inner_row) * SCALE).astype(jnp.bfloat16)
            dk[:, cols] = dot(ds_t, q[:, cols]).astype(jnp.bfloat16)
            dv[:, cols] = dot(p_t.astype(jnp.bfloat16), da_h).astype(jnp.bfloat16)
        stores = [
            store_g,
            move(14, dq, dq_out),
            move(15, dk, dk_out),
            move(16, dv, dv_out),
        ]
        load_w.wait()
        for n in range(0, WIDTH, 256):
            cols = slice(n, n + 256)
            dh[:, cols] = (
                dot_nt(dq[...], wv[0, cols, :])
                + dot_nt(dk[...], wv[1, cols, :])
                + dot_nt(dv[...], wv[2, cols, :])
            )
        load_x.wait()
        load_gain.wait()
        as_float = x[...].astype(jnp.float32)
        rscale = lax.rsqrt(jnp.mean(as_float * as_float, axis=-1, keepdims=True) + 1e-06)
        d_normed = dh[...]
        scaled = gain[0:1, :] * d_normed
        cubic = rscale * rscale * rscale
        frame_f = (
            g[:BLOCK, :].astype(jnp.float32)
            + rscale * scaled
            - as_float * (cubic * jnp.mean(scaled * as_float, axis=-1, keepdims=True))
        )
        frame[...] = frame_f.astype(jnp.bfloat16)
        stores.append(move(17, frame, frame_out))
        term = jnp.sum(d_normed * as_float * rscale, axis=0, keepdims=True)
        gain_sum[...] = jnp.broadcast_to(term, (8, WIDTH))
        stores.append(move(18, gain_sum, gain_out))
        for copy in stores:
            copy.wait()


def backward(micro, flag, incoming, w, kept, x, gain, stash):
    block = jax.ShapeDtypeStruct((BLOCK, WIDTH), jnp.bfloat16)
    outs = [block] * 5 + [jax.ShapeDtypeStruct((8, WIDTH), jnp.float32)]
    first = stash is None
    operands = [flag, *incoming, w, *kept, x, gain] + ([] if first else list(stash))
    anywhere = pl.BlockSpec(memory_space=pl.ANY)
    bf16, f32 = jnp.bfloat16, jnp.float32
    scratch = [
        ((3 * BLOCK, WIDTH), bf16),
        ((4, WIDTH, WIDTH), bf16),
        ((3 * BLOCK, WIDTH), bf16),
        ((3 * BLOCK, WIDTH), bf16),
        ((3 * BLOCK, WIDTH), bf16),
        ((HEADS, BLOCK, 3 * BLOCK), f32),
        ((HEADS, BLOCK, 3 * BLOCK), f32),
        ((3 * BLOCK, WIDTH), f32),
        ((BLOCK, WIDTH), bf16),
        ((8, WIDTH), f32),
        ((3 * BLOCK, WIDTH), bf16),
        ((BLOCK, WIDTH), bf16),
        ((BLOCK, WIDTH), bf16),
        ((BLOCK, WIDTH), bf16),
        ((BLOCK, WIDTH), f32),
        ((BLOCK, WIDTH), bf16),
        ((8, WIDTH), f32),
    ]
    return pl.pallas_call(
        partial(backward_kernel, micro, first),
        in_specs=[pl.BlockSpec(memory_space=pltpu.SMEM)] + [anywhere] * (len(operands) - 1),
        out_specs=[anywhere] * 6,
        out_shape=outs,
        scratch_shapes=[pltpu.VMEM(shape, kind) for shape, kind in scratch]
        + [pltpu.SemaphoreType.DMA((19,))],
        input_output_aliases={} if first else {13 + at: at for at in range(6)},
        compiler_params=pltpu.CompilerParams(vmem_limit_bytes=VMEM_LIMIT),
        cost_estimate=pl.CostEstimate(
            flops=2 * 7 * BLOCK * WIDTH * WIDTH, bytes_accessed=16 << 20, transcendentals=0
        ),
        name="backward",
    )(*operands)


def segments(lengths, block):
    bounds = jnp.cumsum(lengths, axis=1)
    total = lax.axis_size(GROUP) * BLOCK
    places = (block - 2) * BLOCK + jnp.arange(5 * BLOCK, dtype=jnp.int32)
    counted = jnp.sum((places[None, :, None] >= bounds[:, None, :]).astype(jnp.int32), axis=2)
    return jnp.where(places < 0, -1, jnp.where(places >= total, -2, counted))


def body(checkpoints, cotangent, weights, gains, lengths):
    sections, section = lax.axis_size("section"), lax.axis_index("section")
    block = lax.axis_index(GROUP)
    share = gains.shape[1]

    gathered = lax.all_gather(weights[0], GROUP, axis=1, tiled=True)
    spread = lax.dynamic_update_slice(
        jnp.zeros((1, WIDTH), jnp.float32), gains.astype(jnp.float32), (0, block * share)
    )
    gain = jnp.broadcast_to(group_sum(spread), (8, WIDTH))

    x = checkpoints[0]
    left, right = shift(x, 1), shift(x, -1)
    parts = (shift(left, 1), left, x, right, shift(right, -1))
    source = max(sections - 3, 0)
    cot = (cotangent, hop(cotangent, source, sections - 1, 1), hop(cotangent, source, sections - 1, 2))

    segs = segments(lengths, block)
    h, q, k, v, p, pt, o, a = forward(parts, gathered, gain, segs[:, :, None], segs[:, None, :])
    kept = (q, k, v, p, pt, o)

    stash = [None] * MICRO
    incoming = [[part[micro] for part in cot] for micro in range(MICRO)]
    for at in range(sections - 1, -1, -1):
        flag = (section == at).astype(jnp.int32).reshape(1)
        for micro in range(MICRO):
            stash[micro] = backward(
                micro, flag, incoming[micro], gathered, kept, x, gain, stash[micro]
            )
            if at > 0:
                incoming[micro] = [hop(stash[micro][0], at, at - 1, back) for back in range(3)]

    frame, g, dq, dk, dv, gain_part = (
        [stash[micro][at] for micro in range(MICRO)] for at in range(6)
    )
    h, a = h.reshape(-1, WIDTH), a.reshape(-1, WIDTH)
    term = jnp.stack(
        [
            dot_tn(h, jnp.concatenate(dq)),
            dot_tn(h, jnp.concatenate(dk)),
            dot_tn(h, jnp.concatenate(dv)),
            dot_tn(a, jnp.concatenate(g)),
        ]
    )
    weight_part = lax.psum_scatter(
        term.astype(jnp.bfloat16), GROUP, scatter_dimension=1, tiled=True
    ).astype(jnp.float32)
    gain_term = (gain_part[0][0:1] + gain_part[1][0:1]).astype(jnp.bfloat16).astype(jnp.float32)
    gain_sum = lax.dynamic_slice(group_sum(gain_term), (0, block * share), (1, share))
    return (jnp.stack(frame)[None], weight_part[None], gain_sum)


def solution(mesh):
    placed = (
        P("section", None, ("dp", "fsdp"), None),
        P(None, ("dp", "fsdp"), None),
        P("section", None, ("dp", "fsdp"), None),
        P("section", ("dp", "fsdp")),
        P(),
    )
    return jax.shard_map(
        body,
        mesh=mesh,
        in_specs=placed,
        out_specs=(
            P("section", None, ("dp", "fsdp"), None),
            P("section", None, ("dp", "fsdp"), None),
            P("section", ("dp", "fsdp")),
        ),
        check_vma=False,
    )
```

time: 1150 us -> 816 us (0.71)
  starting transfers between devices: 76.1 us -> 407 us
  local copies, waits for them, and re-layouts: 264 us -> 5.68 us
  blocking collectives: 160 us -> 0 us
  waiting for transfers between devices: 457 us -> 313 us
  other arithmetic: 102 us -> 10.7 us
  matrix products: 69.5 us -> 2.97 us
  Pallas kernels: 0 us -> 56.7 us
    ppermute x29 -> x62, starting transfers between devices: 76 us -> 407 us  [the longest x44 370 us: hop(): return lax.ppermute(value, EVERY, pairs)]
    ppermute x29 -> x62, waiting for transfers between devices: 309 us -> 51.6 us  [the longest x14 29 us: turn(): return lax.ppermute(value, GROUP, pairs)]
    dynamic_slice x94 -> x0, local copies, waits for them, and re-layouts: 118 us -> none  [pick_slot(): return lax.dynamic_index_in_dim(array_in, slot_index, 0, keepdims=False)]
    all_gather x1 -> x0, blocking collectives: 81.9 us -> none  [body(): lax.all_gather(gains[0], ('dp', 'fsdp'), axis=0, tiled=True)]
    unnamed x1 -> x0, blocking collectives: 78.4 us -> none
    dot_general x31 -> x4, matrix products: 69.5 us -> 2.97 us  [dot_tn(): lax.dot_general(left, right, (((0,), (0,)), ((), ())), preferred_element_...]
    all_gather x1, waiting for transfers between devices: 45.2 us -> 103 us  [body(): gathered = lax.all_gather(weights[0], GROUP, axis=1, tiled=True)]
    pallas_call x0 -> x17, Pallas kernels: none -> 56.7 us  [the longest x1 32.6 us: forward(): pl.pallas_call(forward_kernel, grid=(MICRO,), in_specs=[per_micro((BLOCK,...]
  transfers between devices with their start and end apart: 31 -> 64, of which waited for: 13 -> 14; matrix products, arithmetic and copies ran while one was open for 12% -> 1% of each run, Pallas kernels for 0% -> 2%
where the time goes in v1:
time: 816 us; the launch traced here: 810 us
  starting transfers between devices  407 us (50%)
  waiting for transfers between devices  313 us (38%)
  Pallas kernels  56.7 us (7%)
  between operations  14.9 us (2%)
  other arithmetic  10.7 us (1%)
    ppermute x44, starting transfers between devices, hop(): return lax.ppermute(value, EVERY, pairs)  370 us
    reduce_scatter x1, waiting for transfers between devices, body(): lax.psum_scatter(term.astype(jnp.bfloat16), GROUP, scatter_dimension=1, t...  157 us
    all_gather x1, waiting for transfers between devices, body(): gathered = lax.all_gather(weights[0], GROUP, axis=1, tiled=True)  103 us
    pallas_call x1, Pallas kernels, forward(): pl.pallas_call(forward_kernel, grid=(MICRO,), in_specs=[per_micro((BLOCK,...  32.6 us
    ppermute x14, waiting for transfers between devices, turn(): return lax.ppermute(value, GROUP, pairs)  29 us
    pallas_call x16, Pallas kernels, backward(): pl.pallas_call(partial(backward_kernel, micro, first), in_specs=[pl.Block...  24.1 us
    ppermute x4, waiting for transfers between devices, shift(): return lax.ppermute(value, GROUP, pairs)  22.5 us
    ppermute x14, starting transfers between devices, turn(): return lax.ppermute(value, GROUP, pairs)  21.3 us
  transfers between devices with their start and end apart: 64, of which 14 were waited for; matrix products, arithmetic and copies ran while one was open for 1% of the time, Pallas kernels for 2%

profile of v1, /device:TPU:32, one launch (start us, length us, event | category | flops | bytes accessed | tf_op | source)
XLA Modules:
  0.0 810.2 jit_solution(7549679216080434810)
XLA Ops:
  18.9 10.1 %collective-permute-done.6 = f32[1,1024]{1,0:T(1,128)S(1)} collective-permute-done((f32[1,1024]{1,0:T(1,128)S(1)}, f32[1,1024]{1,0:T(1,128)S(1)}, u32[]{:S(2)}, u32[]{:S(2)}) %collective-permute-start.6) | collective-permute-done | bytes 4128 | tf_op jit(solution)/shard_map/ppermute | solution.py:68
  61.8 14.9 %collective-permute-done.5.r2 = bf16[2,128,1024]{2,1,0:T(8,128)(2,1)} collective-permute-done((bf16[2,128,1024]{2,1,0:T(8,128)(2,1)}, bf16[2,128,1024]{2,1,0:T(8,128)(2,1)}, u32[]{:S(2)}, u32[]{:S(2)}) %collective-permute-start.5) | collective-permute-done | bytes 524320 | tf_op jit(solution)/shard_map/ppermute | solution.py:37
  84.3 103.0 %all-gather.3.cloned.1.call-done = bf16[1,4,1024,1024]{3,2,1,0:T(8,128)(2,1)} async-done(((bf16[1,4,32,1024]{3,2,1,0:T(8,128)(2,1)}), bf16[1,4,1024,1024]{3,2,1,0:T(8,128)(2,1)}) %all-gather.3.cloned.1.call-update) | async-done | bytes 8388624 | tf_op jit(solution)/shard_map/all_gather | solution.py:302
  187.3 32.6 %forward.1 = (bf16[2,128,1024]{2,1,0:T(8,128)(2,1)S(1)}, bf16[2,384,1024]{2,1,0:T(8,128)(2,1)}, bf16[2,384,1024]{2,1,0:T(8,128)(2,1)}, bf16[2,384,1024]{2,1,0:T(...) custom-call(bf16[2,128,1024]{2,1,0:T(8,128)(2,1)S(1)} %collective-pe, ...), custom_call_target="tpu_custom_call" | custom-call | flops 8053063680 | bytes 29360128 | tf_op jit(solution)/shard_map/forward/pallas_call | solution.py:138
  221.4 18.3 %collective-permute-start.35 = (bf16[128,1024]{1,0:T(8,128)(2,1)S(1)}, bf16[128,1024]{1,0:T(8,128)(2,1)}, u32[]{:S(2)}, u32[]{:S(2)}) collective-permute-start(bf16[128,1024]{1,0:T(8,128)(2,1)S(1)} %get-tuple-element.156.refs_13_), channel_id=1, source_target_pairs={{29,24},{30,25},{31,26},{60,27},{61,56},{62,57},{63,58},{92,59},{9... | collective-permute-start | bytes 786440 | tf_op jit(solution)/shard_map/ppermute | solution.py:48
  239.7 13.2 %collective-permute-start.34 = (bf16[128,1024]{1,0:T(8,128)(2,1)S(1)}, bf16[128,1024]{1,0:T(8,128)(2,1)}, u32[]{:S(2)}, u32[]{:S(2)}) collective-permute-start(bf16[128,1024]{1,0:T(8,128)(2,1)S(1)} %get-tuple-element.156.refs_13_), channel_id=1, source_target_pairs={{28,24},{29,25},{30,26},{31,27},{60,56},{61,57},{62,58},{63,59},{9... | collective-permute-start | bytes 786440 | tf_op jit(solution)/shard_map/ppermute | solution.py:48
  254.5 22.4 %collective-permute-start.14 = (bf16[128,1024]{1,0:T(8,128)(2,1)S(1)}, bf16[128,1024]{1,0:T(8,128)(2,1)}, u32[]{:S(2)}, u32[]{:S(2)}) collective-permute-start(bf16[128,1024]{1,0:T(8,128)(2,1)S(1)} %get-tuple-element.113.refs_13_), channel_id=1, source_target_pairs={{29,24},{30,25},{31,26},{60,27},{61,56},{62,57},{63,58},{92,59},{9... | collective-permute-start | bytes 786440 | tf_op jit(solution)/shard_map/ppermute | solution.py:48
  277.6 13.2 %collective-permute-start.13 = (bf16[128,1024]{1,0:T(8,128)(2,1)S(1)}, bf16[128,1024]{1,0:T(8,128)(2,1)}, u32[]{:S(2)}, u32[]{:S(2)}) collective-permute-start(bf16[128,1024]{1,0:T(8,128)(2,1)S(1)} %get-tuple-element.113.refs_13_), channel_id=1, source_target_pairs={{28,24},{29,25},{30,26},{31,27},{60,56},{61,57},{62,58},{63,59},{9... | collective-permute-start | bytes 786440 | tf_op jit(solution)/shard_map/ppermute | solution.py:48
  292.7 20.7 %collective-permute-start.38 = (bf16[128,1024]{1,0:T(8,128)(2,1)S(1)}, bf16[128,1024]{1,0:T(8,128)(2,1)S(1)}, u32[]{:S(2)}, u32[]{:S(2)}) collective-permute-start(bf16[128,1024]{1,0:T(8,128)(2,1)S(1)} %get-tuple-element.162.refs_13_), channel_id=1, source_target_pairs={{25,20},{26,21},{27,22},{56,23},{57,52},{58,53},{59,54},{88,55},{8... | collective-permute-start | bytes 786440 | tf_op jit(solution)/shard_map/ppermute | solution.py:48
  313.4 13.2 %collective-permute-start.37 = (bf16[128,1024]{1,0:T(8,128)(2,1)S(1)}, bf16[128,1024]{1,0:T(8,128)(2,1)}, u32[]{:S(2)}, u32[]{:S(2)}) collective-permute-start(bf16[128,1024]{1,0:T(8,128)(2,1)S(1)} %get-tuple-element.162.refs_13_), channel_id=1, source_target_pairs={{24,20},{25,21},{26,22},{27,23},{56,52},{57,53},{58,54},{59,55},{8... | collective-permute-start | bytes 786440 | tf_op jit(solution)/shard_map/ppermute | solution.py:48
  329.6 23.3 %collective-permute-start.16 = (bf16[128,1024]{1,0:T(8,128)(2,1)S(1)}, bf16[128,1024]{1,0:T(8,128)(2,1)}, u32[]{:S(2)}, u32[]{:S(2)}) collective-permute-start(bf16[128,1024]{1,0:T(8,128)(2,1)S(1)} %get-tuple-element.119.refs_13_), channel_id=1, source_target_pairs={{24,20},{25,21},{26,22},{27,23},{56,52},{57,53},{58,54},{59,55},{8... | collective-permute-start | bytes 786440 | tf_op jit(solution)/shard_map/ppermute | solution.py:48
  355.4 23.0 %collective-permute-start.40 = (bf16[128,1024]{1,0:T(8,128)(2,1)S(1)}, bf16[128,1024]{1,0:T(8,128)(2,1)}, u32[]{:S(2)}, u32[]{:S(2)}) collective-permute-start(bf16[128,1024]{1,0:T(8,128)(2,1)S(1)} %get-tuple-element.168.refs_13_), channel_id=1, source_target_pairs={{20,16},{21,17},{22,18},{23,19},{52,48},{53,49},{54,50},{55,51},{8... | collective-permute-start | bytes 786440 | tf_op jit(solution)/shard_map/ppermute | solution.py:48
  380.6 23.7 %collective-permute-start.19 = (bf16[128,1024]{1,0:T(8,128)(2,1)S(1)}, bf16[128,1024]{1,0:T(8,128)(2,1)S(1)}, u32[]{:S(2)}, u32[]{:S(2)}) collective-permute-start(bf16[128,1024]{1,0:T(8,128)(2,1)S(1)} %get-tuple-element.125.refs_13_), channel_id=1, source_target_pairs={{20,16},{21,17},{22,18},{23,19},{52,48},{53,49},{54,50},{55,51},{8... | collective-permute-start | bytes 786440 | tf_op jit(solution)/shard_map/ppermute | solution.py:48
  406.1 23.9 %collective-permute-start.43 = (bf16[128,1024]{1,0:T(8,128)(2,1)S(1)}, bf16[128,1024]{1,0:T(8,128)(2,1)}, u32[]{:S(2)}, u32[]{:S(2)}) collective-permute-start(bf16[128,1024]{1,0:T(8,128)(2,1)S(1)} %get-tuple-element.174.refs_13_), channel_id=1, source_target_pairs={{16,12},{17,13},{18,14},{19,15},{48,44},{49,45},{50,46},{51,47},{8... | collective-permute-start | bytes 786440 | tf_op jit(solution)/shard_map/ppermute | solution.py:48
  433.7 24.5 %collective-permute-start.22 = (bf16[128,1024]{1,0:T(8,128)(2,1)S(1)}, bf16[128,1024]{1,0:T(8,128)(2,1)}, u32[]{:S(2)}, u32[]{:S(2)}) collective-permute-start(bf16[128,1024]{1,0:T(8,128)(2,1)S(1)} %get-tuple-element.131.refs_13_), channel_id=1, source_target_pairs={{16,12},{17,13},{18,14},{19,15},{48,44},{49,45},{50,46},{51,47},{8... | collective-permute-start | bytes 786440 | tf_op jit(solution)/shard_map/ppermute | solution.py:48
  460.8 20.6 %collective-permute-start.46 = (bf16[128,1024]{1,0:T(8,128)(2,1)S(1)}, bf16[128,1024]{1,0:T(8,128)(2,1)}, u32[]{:S(2)}, u32[]{:S(2)}) collective-permute-start(bf16[128,1024]{1,0:T(8,128)(2,1)S(1)} %get-tuple-element.180.refs_13_), channel_id=1, source_target_pairs={{12,8},{13,9},{14,10},{15,11},{44,40},{45,41},{46,42},{47,43},{76,... | collective-permute-start | bytes 786440 | tf_op jit(solution)/shard_map/ppermute | solution.py:48
  484.4 22.0 %collective-permute-start.25 = (bf16[128,1024]{1,0:T(8,128)(2,1)S(1)}, bf16[128,1024]{1,0:T(8,128)(2,1)}, u32[]{:S(2)}, u32[]{:S(2)}) collective-permute-start(bf16[128,1024]{1,0:T(8,128)(2,1)S(1)} %get-tuple-element.137.refs_13_), channel_id=1, source_target_pairs={{12,8},{13,9},{14,10},{15,11},{44,40},{45,41},{46,42},{47,43},{76,... | collective-permute-start | bytes 786440 | tf_op jit(solution)/shard_map/ppermute | solution.py:48
  508.7 20.9 %collective-permute-start.49 = (bf16[128,1024]{1,0:T(8,128)(2,1)S(1)}, bf16[128,1024]{1,0:T(8,128)(2,1)}, u32[]{:S(2)}, u32[]{:S(2)}) collective-permute-start(bf16[128,1024]{1,0:T(8,128)(2,1)S(1)} %get-tuple-element.186.refs_13_), channel_id=1, source_target_pairs={{8,4},{9,5},{10,6},{11,7},{40,36},{41,37},{42,38},{43,39},{72,68},... | collective-permute-start | bytes 786440 | tf_op jit(solution)/shard_map/ppermute | solution.py:48
  531.2 21.6 %collective-permute-start.28 = (bf16[128,1024]{1,0:T(8,128)(2,1)S(1)}, bf16[128,1024]{1,0:T(8,128)(2,1)S(1)}, u32[]{:S(2)}, u32[]{:S(2)}) collective-permute-start(bf16[128,1024]{1,0:T(8,128)(2,1)S(1)} %get-tuple-element.143.refs_13_), channel_id=1, source_target_pairs={{8,4},{9,5},{10,6},{11,7},{40,36},{41,37},{42,38},{43,39},{72,68},... | collective-permute-start | bytes 786440 | tf_op jit(solution)/shard_map/ppermute | solution.py:48
  555.8 16.9 %collective-permute-start.52 = (bf16[128,1024]{1,0:T(8,128)(2,1)S(1)}, bf16[128,1024]{1,0:T(8,128)(2,1)}, u32[]{:S(2)}, u32[]{:S(2)}) collective-permute-start(bf16[128,1024]{1,0:T(8,128)(2,1)S(1)} %get-tuple-element.192.refs_13_), channel_id=1, source_target_pairs={{4,0},{5,1},{6,2},{7,3},{36,32},{37,33},{38,34},{39,35},{68,64},{6... | collective-permute-start | bytes 786440 | tf_op jit(solution)/shard_map/ppermute | solution.py:48
  576.3 19.7 %collective-permute-start.31 = (bf16[128,1024]{1,0:T(8,128)(2,1)S(1)}, bf16[128,1024]{1,0:T(8,128)(2,1)}, u32[]{:S(2)}, u32[]{:S(2)}) collective-permute-start(bf16[128,1024]{1,0:T(8,128)(2,1)S(1)} %get-tuple-element.149.refs_13_), channel_id=1, source_target_pairs={{4,0},{5,1},{6,2},{7,3},{36,32},{37,33},{38,34},{39,35},{68,64},{6... | collective-permute-start | bytes 786440 | tf_op jit(solution)/shard_map/ppermute | solution.py:48
  595.9 10.0 %backward.31 = (bf16[128,1024]{1,0:T(8,128)(2,1)S(1)}, bf16[128,1024]{1,0:T(8,128)(2,1)S(1)}, bf16[128,1024]{1,0:T(8,128)(2,1)S(1)}, bf16[128,1024]{1,0:T(8,128)...) custom-call(s32[1]{0:T(128)} %bitcast.refs_0_, ...), custom_call_target="tpu_custom_call", output_to_operand_aliasing={{0}: (13, {}), {1}: (14, {}), {2}: (15, {}), {3}: (16, {}),... | custom-call | flops 1879048192 | bytes 16777216 | tf_op jit(solution)/shard_map/backward/pallas_call | solution.py:273
  606.0 9.9 %backward.23 = (bf16[128,1024]{1,0:T(8,128)(2,1)S(1)}, bf16[128,1024]{1,0:T(8,128)(2,1)S(1)}, bf16[128,1024]{1,0:T(8,128)(2,1)S(1)}, bf16[128,1024]{1,0:T(8,128)...) custom-call(s32[1]{0:T(128)} %bitcast.refs_0_, ...), custom_call_target="tpu_custom_call", output_to_operand_aliasing={{0}: (13, {}), {1}: (14, {}), {2}: (15, {}), {3}: (16, {}),... | custom-call | flops 1879048192 | bytes 16777216 | tf_op jit(solution)/shard_map/backward/pallas_call | solution.py:273
  644.1 157.3 %reduce-scatter.2.cloned.1.call-done = bf16[4,32,1024]{2,1,0:T(8,128)(2,1)} async-done(((bf16[4,1024,1024]{2,1,0:T(8,128)(2,1)}), bf16[4,32,1024]{2,1,0:T(8,128)(2,1)}) %reduce-scatter.2.cloned.1.call-update) | async-done | bytes 262160 | tf_op jit(solution)/shard_map/reduce_scatter | solution.py:341
  (169 shorter events, 116.4 us)
Async XLA Ops:
  7.2 180.2 %all-gather.3.cloned.1.call-start = ((), (), s32[]{:S(2)}) async-start(), calls=%async_computation.2 | async-start | bytes 8650752 | tf_op jit(solution)/shard_map/all_gather | solution.py:302
  7.9 793.4 %reduce-scatter.2.cloned.1.call-start = ((), (), s32[]{:S(2)}) async-start(), calls=%async_computation.1 | async-start | bytes 8650752 | tf_op jit(solution)/shard_map/reduce_scatter | solution.py:341
  8.0 45.9 %collective-permute-start.4 = (bf16[2,128,1024]{2,1,0:T(8,128)(2,1)}, bf16[2,128,1024]{2,1,0:T(8,128)(2,1)}, u32[]{:S(2)}, u32[]{:S(2)}) collective-permute-start(bf16[2,128,1024]{2,1,0:T(8,128)(2,1)} %bitcast.68), channel_id=1, source_target_pairs={{1,0},{2,1},{3,2},{32,3},{33,32},{34,33},{35,34},{64,35},{65,64},{... | collective-permute-start | bytes 1572872 | tf_op jit(solution)/shard_map/ppermute | solution.py:37
  220.7 56.2 %collective-permute-start.36 = (bf16[128,1024]{1,0:T(8,128)(2,1)S(1)}, bf16[128,1024]{1,0:T(8,128)(2,1)S(1)}, u32[]{:S(2)}, u32[]{:S(2)}) collective-permute-start(bf16[128,1024]{1,0:T(8,128)(2,1)S(1)} %get-tuple-element.156.refs_13_), channel_id=1, source_target_pairs={{30,24},{31,25},{60,26},{61,27},{62,56},{63,57},{92,58},{93,59},{9... | collective-permute-start | bytes 786440 | tf_op jit(solution)/shard_map/ppermute | solution.py:48
  221.4 69.4 %collective-permute-start.35 = (bf16[128,1024]{1,0:T(8,128)(2,1)S(1)}, bf16[128,1024]{1,0:T(8,128)(2,1)}, u32[]{:S(2)}, u32[]{:S(2)}) collective-permute-start(bf16[128,1024]{1,0:T(8,128)(2,1)S(1)} %get-tuple-element.156.refs_13_), channel_id=1, source_target_pairs={{29,24},{30,25},{31,26},{60,27},{61,56},{62,57},{63,58},{92,59},{9... | collective-permute-start | bytes 786440 | tf_op jit(solution)/shard_map/ppermute | solution.py:48
  239.7 51.1 %collective-permute-start.34 = (bf16[128,1024]{1,0:T(8,128)(2,1)S(1)}, bf16[128,1024]{1,0:T(8,128)(2,1)}, u32[]{:S(2)}, u32[]{:S(2)}) collective-permute-start(bf16[128,1024]{1,0:T(8,128)(2,1)S(1)} %get-tuple-element.156.refs_13_), channel_id=1, source_target_pairs={{28,24},{29,25},{30,26},{31,27},{60,56},{61,57},{62,58},{63,59},{9... | collective-permute-start | bytes 786440 | tf_op jit(solution)/shard_map/ppermute | solution.py:48
  253.1 60.3 %collective-permute-start.15 = (bf16[128,1024]{1,0:T(8,128)(2,1)S(1)}, bf16[128,1024]{1,0:T(8,128)(2,1)}, u32[]{:S(2)}, u32[]{:S(2)}) collective-permute-start(bf16[128,1024]{1,0:T(8,128)(2,1)S(1)} %get-tuple-element.113.refs_13_), channel_id=1, source_target_pairs={{30,24},{31,25},{60,26},{61,27},{62,56},{63,57},{92,58},{93,59},{9... | collective-permute-start | bytes 786440 | tf_op jit(solution)/shard_map/ppermute | solution.py:48
  254.5 72.1 %collective-permute-start.14 = (bf16[128,1024]{1,0:T(8,128)(2,1)S(1)}, bf16[128,1024]{1,0:T(8,128)(2,1)}, u32[]{:S(2)}, u32[]{:S(2)}) collective-permute-start(bf16[128,1024]{1,0:T(8,128)(2,1)S(1)} %get-tuple-element.113.refs_13_), channel_id=1, source_target_pairs={{29,24},{30,25},{31,26},{60,27},{61,56},{62,57},{63,58},{92,59},{9... | collective-permute-start | bytes 786440 | tf_op jit(solution)/shard_map/ppermute | solution.py:48
  277.6 49.0 %collective-permute-start.13 = (bf16[128,1024]{1,0:T(8,128)(2,1)S(1)}, bf16[128,1024]{1,0:T(8,128)(2,1)}, u32[]{:S(2)}, u32[]{:S(2)}) collective-permute-start(bf16[128,1024]{1,0:T(8,128)(2,1)S(1)} %get-tuple-element.113.refs_13_), channel_id=1, source_target_pairs={{28,24},{29,25},{30,26},{31,27},{60,56},{61,57},{62,58},{63,59},{9... | collective-permute-start | bytes 786440 | tf_op jit(solution)/shard_map/ppermute | solution.py:48
  292.7 60.3 %collective-permute-start.38 = (bf16[128,1024]{1,0:T(8,128)(2,1)S(1)}, bf16[128,1024]{1,0:T(8,128)(2,1)S(1)}, u32[]{:S(2)}, u32[]{:S(2)}) collective-permute-start(bf16[128,1024]{1,0:T(8,128)(2,1)S(1)} %get-tuple-element.162.refs_13_), channel_id=1, source_target_pairs={{25,20},{26,21},{27,22},{56,23},{57,52},{58,53},{59,54},{88,55},{8... | collective-permute-start | bytes 786440 | tf_op jit(solution)/shard_map/ppermute | solution.py:48
  328.3 50.1 %collective-permute-start.17 = (bf16[128,1024]{1,0:T(8,128)(2,1)S(1)}, bf16[128,1024]{1,0:T(8,128)(2,1)}, u32[]{:S(2)}, u32[]{:S(2)}) collective-permute-start(bf16[128,1024]{1,0:T(8,128)(2,1)S(1)} %get-tuple-element.119.refs_13_), channel_id=1, source_target_pairs={{25,20},{26,21},{27,22},{56,23},{57,52},{58,53},{59,54},{88,55},{8... | collective-permute-start | bytes 786440 | tf_op jit(solution)/shard_map/ppermute | solution.py:48
  329.6 48.7 %collective-permute-start.16 = (bf16[128,1024]{1,0:T(8,128)(2,1)S(1)}, bf16[128,1024]{1,0:T(8,128)(2,1)}, u32[]{:S(2)}, u32[]{:S(2)}) collective-permute-start(bf16[128,1024]{1,0:T(8,128)(2,1)S(1)} %get-tuple-element.119.refs_13_), channel_id=1, source_target_pairs={{24,20},{25,21},{26,22},{27,23},{56,52},{57,53},{58,54},{59,55},{8... | collective-permute-start | bytes 786440 | tf_op jit(solution)/shard_map/ppermute | solution.py:48
  354.7 49.6 %collective-permute-start.41 = (bf16[128,1024]{1,0:T(8,128)(2,1)S(1)}, bf16[128,1024]{1,0:T(8,128)(2,1)S(1)}, u32[]{:S(2)}, u32[]{:S(2)}) collective-permute-start(bf16[128,1024]{1,0:T(8,128)(2,1)S(1)} %get-tuple-element.168.refs_13_), channel_id=1, source_target_pairs={{21,16},{22,17},{23,18},{52,19},{53,48},{54,49},{55,50},{84,51},{8... | collective-permute-start | bytes 786440 | tf_op jit(solution)/shard_map/ppermute | solution.py:48
  355.4 48.9 %collective-permute-start.40 = (bf16[128,1024]{1,0:T(8,128)(2,1)S(1)}, bf16[128,1024]{1,0:T(8,128)(2,1)}, u32[]{:S(2)}, u32[]{:S(2)}) collective-permute-start(bf16[128,1024]{1,0:T(8,128)(2,1)S(1)} %get-tuple-element.168.refs_13_), channel_id=1, source_target_pairs={{20,16},{21,17},{22,18},{23,19},{52,48},{53,49},{54,50},{55,51},{8... | collective-permute-start | bytes 786440 | tf_op jit(solution)/shard_map/ppermute | solution.py:48
  379.9 50.1 %collective-permute-start.20 = (bf16[128,1024]{1,0:T(8,128)(2,1)S(1)}, bf16[128,1024]{1,0:T(8,128)(2,1)S(1)}, u32[]{:S(2)}, u32[]{:S(2)}) collective-permute-start(bf16[128,1024]{1,0:T(8,128)(2,1)S(1)} %get-tuple-element.125.refs_13_), channel_id=1, source_target_pairs={{21,16},{22,17},{23,18},{52,19},{53,48},{54,49},{55,50},{84,51},{8... | collective-permute-start | bytes 786440 | tf_op jit(solution)/shard_map/ppermute | solution.py:48
  380.6 49.4 %collective-permute-start.19 = (bf16[128,1024]{1,0:T(8,128)(2,1)S(1)}, bf16[128,1024]{1,0:T(8,128)(2,1)S(1)}, u32[]{:S(2)}, u32[]{:S(2)}) collective-permute-start(bf16[128,1024]{1,0:T(8,128)(2,1)S(1)} %get-tuple-element.125.refs_13_), channel_id=1, source_target_pairs={{20,16},{21,17},{22,18},{23,19},{52,48},{53,49},{54,50},{55,51},{8... | collective-permute-start | bytes 786440 | tf_op jit(solution)/shard_map/ppermute | solution.py:48
  405.4 52.8 %collective-permute-start.44 = (bf16[128,1024]{1,0:T(8,128)(2,1)S(1)}, bf16[128,1024]{1,0:T(8,128)(2,1)S(1)}, u32[]{:S(2)}, u32[]{:S(2)}) collective-permute-start(bf16[128,1024]{1,0:T(8,128)(2,1)S(1)} %get-tuple-element.174.refs_13_), channel_id=1, source_target_pairs={{17,12},{18,13},{19,14},{48,15},{49,44},{50,45},{51,46},{80,47},{8... | collective-permute-start | bytes 786440 | tf_op jit(solution)/shard_map/ppermute | solution.py:48
  406.1 52.1 %collective-permute-start.43 = (bf16[128,1024]{1,0:T(8,128)(2,1)S(1)}, bf16[128,1024]{1,0:T(8,128)(2,1)}, u32[]{:S(2)}, u32[]{:S(2)}) collective-permute-start(bf16[128,1024]{1,0:T(8,128)(2,1)S(1)} %get-tuple-element.174.refs_13_), channel_id=1, source_target_pairs={{16,12},{17,13},{18,14},{19,15},{48,44},{49,45},{50,46},{51,47},{8... | collective-permute-start | bytes 786440 | tf_op jit(solution)/shard_map/ppermute | solution.py:48
  431.6 49.8 %collective-permute-start.23 = (bf16[128,1024]{1,0:T(8,128)(2,1)S(1)}, bf16[128,1024]{1,0:T(8,128)(2,1)}, u32[]{:S(2)}, u32[]{:S(2)}) collective-permute-start(bf16[128,1024]{1,0:T(8,128)(2,1)S(1)} %get-tuple-element.131.refs_13_), channel_id=1, source_target_pairs={{17,12},{18,13},{19,14},{48,15},{49,44},{50,45},{51,46},{80,47},{8... | collective-permute-start | bytes 786440 | tf_op jit(solution)/shard_map/ppermute | solution.py:48
  433.7 47.7 %collective-permute-start.22 = (bf16[128,1024]{1,0:T(8,128)(2,1)S(1)}, bf16[128,1024]{1,0:T(8,128)(2,1)}, u32[]{:S(2)}, u32[]{:S(2)}) collective-permute-start(bf16[128,1024]{1,0:T(8,128)(2,1)S(1)} %get-tuple-element.131.refs_13_), channel_id=1, source_target_pairs={{16,12},{17,13},{18,14},{19,15},{48,44},{49,45},{50,46},{51,47},{8... | collective-permute-start | bytes 786440 | tf_op jit(solution)/shard_map/ppermute | solution.py:48
  460.1 46.3 %collective-permute-start.47 = (bf16[128,1024]{1,0:T(8,128)(2,1)S(1)}, bf16[128,1024]{1,0:T(8,128)(2,1)S(1)}, u32[]{:S(2)}, u32[]{:S(2)}) collective-permute-start(bf16[128,1024]{1,0:T(8,128)(2,1)S(1)} %get-tuple-element.180.refs_13_), channel_id=1, source_target_pairs={{13,8},{14,9},{15,10},{44,11},{45,40},{46,41},{47,42},{76,43},{77,... | collective-permute-start | bytes 786440 | tf_op jit(solution)/shard_map/ppermute | solution.py:48
  460.8 45.6 %collective-permute-start.46 = (bf16[128,1024]{1,0:T(8,128)(2,1)S(1)}, bf16[128,1024]{1,0:T(8,128)(2,1)}, u32[]{:S(2)}, u32[]{:S(2)}) collective-permute-start(bf16[128,1024]{1,0:T(8,128)(2,1)S(1)} %get-tuple-element.180.refs_13_), channel_id=1, source_target_pairs={{12,8},{13,9},{14,10},{15,11},{44,40},{45,41},{46,42},{47,43},{76,... | collective-permute-start | bytes 786440 | tf_op jit(solution)/shard_map/ppermute | solution.py:48
  483.0 46.6 %collective-permute-start.26 = (bf16[128,1024]{1,0:T(8,128)(2,1)S(1)}, bf16[128,1024]{1,0:T(8,128)(2,1)}, u32[]{:S(2)}, u32[]{:S(2)}) collective-permute-start(bf16[128,1024]{1,0:T(8,128)(2,1)S(1)} %get-tuple-element.137.refs_13_), channel_id=1, source_target_pairs={{13,8},{14,9},{15,10},{44,11},{45,40},{46,41},{47,42},{76,43},{77,... | collective-permute-start | bytes 786440 | tf_op jit(solution)/shard_map/ppermute | solution.py:48
  484.4 45.2 %collective-permute-start.25 = (bf16[128,1024]{1,0:T(8,128)(2,1)S(1)}, bf16[128,1024]{1,0:T(8,128)(2,1)}, u32[]{:S(2)}, u32[]{:S(2)}) collective-permute-start(bf16[128,1024]{1,0:T(8,128)(2,1)S(1)} %get-tuple-element.137.refs_13_), channel_id=1, source_target_pairs={{12,8},{13,9},{14,10},{15,11},{44,40},{45,41},{46,42},{47,43},{76,... | collective-permute-start | bytes 786440 | tf_op jit(solution)/shard_map/ppermute | solution.py:48
  (48 other events, 1012.9 us)
Sparse Core Ops, SparseCore 0:
  9.8 177.4 all-gather.2
  623.0 178.2 reduce-scatter.1

commit v2 on v1

--- a/solution.py
+++ b/solution.py
@@ -70,7 +70,10 @@
 
 def group_sum(value):
     for axis, size in enumerate(group_dims()):
-        value = sum([turn(value, axis, steps) for steps in range(1, size)], value)
+        moving = value
+        for _ in range(size - 1):
+            moving = turn(moving, axis, 1)
+            value = value + moving
     return value
 
 
@@ -286,6 +289,22 @@
     )(*operands)
 
 
+def tie_kernel(*refs):
+    del refs
+
+
+def tie(value, *others):
+    anywhere = pl.BlockSpec(memory_space=pl.ANY)
+    return pl.pallas_call(
+        tie_kernel,
+        in_specs=[anywhere] * (1 + len(others)),
+        out_specs=anywhere,
+        out_shape=jax.ShapeDtypeStruct(value.shape, value.dtype),
+        input_output_aliases={0: 0},
+        name="tie",
+    )(value, *others)
+
+
 def segments(lengths, block):
     bounds = jnp.cumsum(lengths, axis=1)
     total = lax.axis_size(GROUP) * BLOCK
@@ -320,10 +339,12 @@
     for at in range(sections - 1, -1, -1):
         flag = (section == at).astype(jnp.int32).reshape(1)
         for micro in range(MICRO):
-            stash[micro] = backward(
-                micro, flag, incoming[micro], gathered, kept, x, gain, stash[micro]
+            stash[micro] = list(
+                backward(micro, flag, incoming[micro], gathered, kept, x, gain, stash[micro])
             )
             if at > 0:
+                if micro > 0:
+                    stash[micro][0] = tie(stash[micro][0], *incoming[micro - 1])
                 incoming[micro] = [hop(stash[micro][0], at, at - 1, back) for back in range(3)]
 
     frame, g, dq, dk, dv, gain_part = (

time: 816 us -> 664 us (0.81)
  starting transfers between devices: 407 us -> 94.2 us
  waiting for transfers between devices: 313 us -> 440 us
  local copies, waits for them, and re-layouts: 5.68 us -> 36.3 us
    ppermute x44, starting transfers between devices: 370 us -> 37.6 us  [hop(): return lax.ppermute(value, EVERY, pairs)]
    ppermute x44, waiting for transfers between devices: 0.12 us -> 126 us  [hop(): return lax.ppermute(value, EVERY, pairs)]
    unnamed x16 -> x122, local copies, waits for them, and re-layouts: 2.5 us -> 32.5 us
    ppermute x14, waiting for transfers between devices: 29 us -> 46.5 us  [turn(): return lax.ppermute(value, GROUP, pairs)]
    ppermute x14, starting transfers between devices: 21.3 us -> 36.3 us  [turn(): return lax.ppermute(value, GROUP, pairs)]
    reduce_scatter x1, waiting for transfers between devices: 157 us -> 144 us  [body(): lax.psum_scatter(term.astype(jnp.bfloat16), GROUP, scatter_dimension=1, t...]
  transfers between devices with their start and end apart: 64 -> 64, of which waited for: 14 -> 20; matrix products, arithmetic and copies ran while one was open for 1% -> 1% of each run, Pallas kernels for 2% -> 2%
where the time goes in v2:
time: 664 us; the launch traced here: 656 us
  waiting for transfers between devices  440 us (66%)
  starting transfers between devices  94.2 us (14%)
  Pallas kernels  56.4 us (8%)
  local copies, waits for them, and re-layouts  36.3 us (5%)
  between operations  15.4 us (2%)
  other arithmetic  10.8 us (2%)
    reduce_scatter x1, waiting for transfers between devices, body(): lax.psum_scatter(term.astype(jnp.bfloat16), GROUP, scatter_dimension=1, t...  144 us
    ppermute x44, waiting for transfers between devices, hop(): return lax.ppermute(value, EVERY, pairs)  126 us
    all_gather x1, waiting for transfers between devices, body(): gathered = lax.all_gather(weights[0], GROUP, axis=1, tiled=True)  105 us
    ppermute x14, waiting for transfers between devices, turn(): return lax.ppermute(value, GROUP, pairs)  46.5 us
    ppermute x44, starting transfers between devices, hop(): return lax.ppermute(value, EVERY, pairs)  37.6 us
    ppermute x14, starting transfers between devices, turn(): return lax.ppermute(value, GROUP, pairs)  36.3 us
    pallas_call x1, Pallas kernels, forward(): pl.pallas_call(forward_kernel, grid=(MICRO,), in_specs=[per_micro((BLOCK,...  32.6 us
    unnamed x122, local copies, waits for them, and re-layouts  32.5 us
  transfers between devices with their start and end apart: 64, of which 20 were waited for; matrix products, arithmetic and copies ran while one was open for 1% of the time, Pallas kernels for 2%

profile of v2, /device:TPU:32, one launch (start us, length us, event | category | flops | bytes accessed | tf_op | source)
XLA Modules:
  0.0 656.2 jit_solution(16514476192395233256)
XLA Ops:
  14.0 8.1 %collective-permute-start.4 = (bf16[2,128,1024]{2,1,0:T(8,128)(2,1)}, bf16[2,128,1024]{2,1,0:T(8,128)(2,1)S(1)}, u32[]{:S(2)}, u32[]{:S(2)}) collective-permute-start(bf16[2,128,1024]{2,1,0:T(8,128)(2,1)} %bitcast.69), channel_id=1, source_target_pairs={{1,0},{2,1},{3,2},{32,3},{33,32},{34,33},{35,34},{64,35},{65,64},{... | collective-permute-start | bytes 1572872 | tf_op jit(solution)/shard_map/ppermute | solution.py:37
  24.1 4.1 collective-permute-done.7
  28.4 7.4 %collective-permute-done.8 = f32[1,1024]{1,0:T(1,128)S(1)} collective-permute-done((f32[1,1024]{1,0:T(1,128)S(1)}, f32[1,1024]{1,0:T(1,128)S(1)}, u32[]{:S(2)}, u32[]{:S(2)}) %collective-permute-start.8) | collective-permute-done | bytes 4128 | tf_op jit(solution)/shard_map/ppermute | solution.py:68
  36.0 4.8 collective-permute-done.9
  42.0 3.7 collective-permute-done.10
  47.4 3.0 collective-permute-done.11
  52.5 8.3 %collective-permute-start.5 = (bf16[2,128,1024]{2,1,0:T(8,128)(2,1)S(1)}, bf16[2,128,1024]{2,1,0:T(8,128)(2,1)}, u32[]{:S(2)}, u32[]{:S(2)}) collective-permute-start(bf16[2,128,1024]{2,1,0:T(8,128)(2,1)S(1)} %collective-permute-done.4.r1), channel_id=1, source_target_pairs={{1,0},{2,1},{3,2},{32,3},{33,32},{34,33},{35,34},{64,35},{65,64},{... | collective-permute-start | bytes 1572872 | tf_op jit(solution)/shard_map/ppermute | solution.py:37
  62.4 17.6 %collective-permute-done.3.l2 = bf16[2,128,1024]{2,1,0:T(8,128)(2,1)S(1)} collective-permute-done((bf16[2,128,1024]{2,1,0:T(8,128)(2,1)S(1)}, bf16[2,128,1024]{2,1,0:T(8,128)(2,1)S(1)}, u32[]{:S(2)}, u32[]{:S(2)}) %collective-permute-start.3) | collective-permute-done | bytes 524320 | tf_op jit(solution)/shard_map/ppermute | solution.py:37
  81.0 104.7 %all-gather.3.cloned.1.call-done = bf16[1,4,1024,1024]{3,2,1,0:T(8,128)(2,1)} async-done(((bf16[1,4,32,1024]{3,2,1,0:T(8,128)(2,1)}), bf16[1,4,1024,1024]{3,2,1,0:T(8,128)(2,1)}) %all-gather.3.cloned.1.call-update) | async-done | bytes 8388624 | tf_op jit(solution)/shard_map/all_gather | solution.py:321
  185.7 32.6 %forward.1 = (bf16[2,128,1024]{2,1,0:T(8,128)(2,1)S(1)}, bf16[2,384,1024]{2,1,0:T(8,128)(2,1)}, bf16[2,384,1024]{2,1,0:T(8,128)(2,1)}, bf16[2,384,1024]{2,1,0:T(...) custom-call(bf16[2,128,1024]{2,1,0:T(8,128)(2,1)S(1)} %collective-pe, ...), custom_call_target="tpu_custom_call" | custom-call | flops 8053063680 | bytes 29360128 | tf_op jit(solution)/shard_map/forward/pallas_call | solution.py:141
  285.0 116.4 %collective-permute-done.31.refs_1_ = bf16[128,1024]{1,0:T(8,128)(2,1)S(1)} collective-permute-done((bf16[128,1024]{1,0:T(8,128)(2,1)S(1)}, bf16[128,1024]{1,0:T(8,128)(2,1)S(1)}, u32[]{:S(2)}, u32[]{:S(2)}) %collective-permute-start.31) | collective-permute-done | bytes 262176 | tf_op jit(solution)/shard_map/ppermute | solution.py:48
  401.5 6.7 %collective-permute-done.32.refs_2_ = bf16[128,1024]{1,0:T(8,128)(2,1)S(1)} collective-permute-done((bf16[128,1024]{1,0:T(8,128)(2,1)S(1)}, bf16[128,1024]{1,0:T(8,128)(2,1)S(1)}, u32[]{:S(2)}, u32[]{:S(2)}) %collective-permute-start.32) | collective-permute-done | bytes 262176 | tf_op jit(solution)/shard_map/ppermute | solution.py:48
  415.5 10.0 %backward.23 = (bf16[128,1024]{1,0:T(8,128)(2,1)S(1)}, bf16[128,1024]{1,0:T(8,128)(2,1)S(1)}, bf16[128,1024]{1,0:T(8,128)(2,1)S(1)}, bf16[128,1024]{1,0:T(8,128)...) custom-call(s32[1]{0:T(128)} %bitcast.refs_0_, ...), custom_call_target="tpu_custom_call", output_to_operand_aliasing={{0}: (13, {}), {1}: (14, {}), {2}: (15, {}), {3}: (16, {}),... | custom-call | flops 1879048192 | bytes 16777216 | tf_op jit(solution)/shard_map/backward/pallas_call | solution.py:276
  427.5 9.8 %backward.31 = (bf16[128,1024]{1,0:T(8,128)(2,1)S(1)}, bf16[128,1024]{1,0:T(8,128)(2,1)S(1)}, bf16[128,1024]{1,0:T(8,128)(2,1)S(1)}, bf16[128,1024]{1,0:T(8,128)...) custom-call(s32[1]{0:T(128)} %bitcast.refs_0_, ...), custom_call_target="tpu_custom_call", output_to_operand_aliasing={{0}: (13, {}), {1}: (14, {}), {2}: (15, {}), {3}: (16, {}),... | custom-call | flops 1879048192 | bytes 16777216 | tf_op jit(solution)/shard_map/backward/pallas_call | solution.py:276
  440.4 4.0 pad_maximum_fusion
  444.4 27.0 %collective-permute-start.55 = (f32[1,1024]{1,0:T(1,128)S(1)}, f32[1,1024]{1,0:T(1,128)S(1)}, u32[]{:S(2)}, u32[]{:S(2)}) collective-permute-start(f32[1,1024]{1,0:T(1,128)S(1)} %convert_convert_fusion), channel_id=1, source_target_pairs={{0,128},{1,129},{2,130},{3,131},{32,160},{33,161},{34,162},{35,163... | collective-permute-start | bytes 12296 | tf_op jit(solution)/shard_map/ppermute | solution.py:68
  473.0 4.8 collective-permute-done.56
  477.8 5.2 collective-permute-done.57
  483.0 5.2 collective-permute-done.58
  488.2 3.8 collective-permute-start.59
  493.3 2.3 collective-permute-start.60
  495.6 2.5 collective-permute-done.60
  500.1 2.9 collective-permute-done.61
  503.5 143.8 %reduce-scatter.2.cloned.1.call-done = bf16[4,32,1024]{2,1,0:T(8,128)(2,1)} async-done(((bf16[4,1024,1024]{2,1,0:T(8,128)(2,1)}), bf16[4,32,1024]{2,1,0:T(8,128)(2,1)}) %reduce-scatter.2.cloned.1.call-update) | async-done | bytes 262160 | tf_op jit(solution)/shard_map/reduce_scatter | solution.py:362
  (282 shorter events, 102.1 us)
Async XLA Ops:
  7.2 178.5 %all-gather.3.cloned.1.call-start = ((), (), s32[]{:S(2)}) async-start(), calls=%async_computation.2 | async-start | bytes 8650752 | tf_op jit(solution)/shard_map/all_gather | solution.py:321
  7.9 639.5 %reduce-scatter.2.cloned.1.call-start = ((), (), s32[]{:S(2)}) async-start(), calls=%async_computation.1 | async-start | bytes 8650752 | tf_op jit(solution)/shard_map/reduce_scatter | solution.py:362
  8.7 13.4 %collective-permute-start.6 = (f32[1,1024]{1,0:T(1,128)S(1)}, f32[1,1024]{1,0:T(1,128)S(1)}, u32[]{:S(2)}, u32[]{:S(2)}) collective-permute-start(f32[1,1024]{1,0:T(1,128)S(1)} %dynamic_update_slice.5), channel_id=1, source_target_pairs={{0,128},{1,129},{2,130},{3,131},{32,160},{33,161},{34,162},{35,163... | collective-permute-start | bytes 12296 | tf_op jit(solution)/shard_map/ppermute | solution.py:68
  10.6 50.2 %collective-permute-start = (bf16[2,128,1024]{2,1,0:T(8,128)(2,1)}, bf16[2,128,1024]{2,1,0:T(8,128)(2,1)S(1)}, u32[]{:S(2)}, u32[]{:S(2)}) collective-permute-start(bf16[2,128,1024]{2,1,0:T(8,128)(2,1)} %param.6), channel_id=1, source_target_pairs={{21,28},{22,29},{23,30},{52,31},{53,60},{54,61},{55,62},{84,63},{8... | collective-permute-start | bytes 1572872 | tf_op jit(solution)/shard_map/ppermute | solution.py:48
  11.3 50.2 %collective-permute-start.1 = (bf16[2,128,1024]{2,1,0:T(8,128)(2,1)}, bf16[2,128,1024]{2,1,0:T(8,128)(2,1)S(1)}, u32[]{:S(2)}, u32[]{:S(2)}) collective-permute-start(bf16[2,128,1024]{2,1,0:T(8,128)(2,1)} %param.6), channel_id=1, source_target_pairs={{22,28},{23,29},{52,30},{53,31},{54,60},{55,61},{84,62},{85,63},{8... | collective-permute-start | bytes 1572872 | tf_op jit(solution)/shard_map/ppermute | solution.py:48
  12.0 38.5 %collective-permute-start.2 = (bf16[2,128,1024]{2,1,0:T(8,128)(2,1)}, bf16[2,128,1024]{2,1,0:T(8,128)(2,1)S(1)}, u32[]{:S(2)}, u32[]{:S(2)}) collective-permute-start(bf16[2,128,1024]{2,1,0:T(8,128)(2,1)} %bitcast.68), channel_id=1, source_target_pairs={{0,1},{1,2},{2,3},{3,32},{32,33},{33,34},{34,35},{35,64},{64,65},{... | collective-permute-start | bytes 1572872 | tf_op jit(solution)/shard_map/ppermute | solution.py:37
  14.0 38.5 %collective-permute-start.4 = (bf16[2,128,1024]{2,1,0:T(8,128)(2,1)}, bf16[2,128,1024]{2,1,0:T(8,128)(2,1)S(1)}, u32[]{:S(2)}, u32[]{:S(2)}) collective-permute-start(bf16[2,128,1024]{2,1,0:T(8,128)(2,1)} %bitcast.69), channel_id=1, source_target_pairs={{1,0},{2,1},{3,2},{32,3},{33,32},{34,33},{35,34},{64,35},{65,64},{... | collective-permute-start | bytes 1572872 | tf_op jit(solution)/shard_map/ppermute | solution.py:37
  28.2 7.5 %collective-permute-start.8 = (f32[1,1024]{1,0:T(1,128)S(1)}, f32[1,1024]{1,0:T(1,128)S(1)}, u32[]{:S(2)}, u32[]{:S(2)}) collective-permute-start(f32[1,1024]{1,0:T(1,128)S(1)} %collective-permute-done.7), channel_id=1, source_target_pairs={{0,32},{1,33},{2,34},{3,35},{32,64},{33,65},{34,66},{35,67},{64,96... | collective-permute-start | bytes 12296 | tf_op jit(solution)/shard_map/ppermute | solution.py:68
  50.5 10.3 %collective-permute-start.12 = (f32[1,1024]{1,0:T(1,128)S(1)}, f32[1,1024]{1,0:T(1,128)S(1)}, u32[]{:S(2)}, u32[]{:S(2)}) collective-permute-start(f32[1,1024]{1,0:T(1,128)S(1)} %collective-permute-done.11), channel_id=1, source_target_pairs={{0,1},{1,2},{2,3},{3,0},{32,33},{33,34},{34,35},{35,32},{64,65},{6... | collective-permute-start | bytes 12296 | tf_op jit(solution)/shard_map/ppermute | solution.py:68
  50.5 29.5 %collective-permute-start.3 = (bf16[2,128,1024]{2,1,0:T(8,128)(2,1)S(1)}, bf16[2,128,1024]{2,1,0:T(8,128)(2,1)S(1)}, u32[]{:S(2)}, u32[]{:S(2)}) collective-permute-start(bf16[2,128,1024]{2,1,0:T(8,128)(2,1)S(1)} %collective-permute-done.2.l1), channel_id=1, source_target_pairs={{0,1},{1,2},{2,3},{3,32},{32,33},{33,34},{34,35},{35,64},{64,65},{... | collective-permute-start | bytes 1572872 | tf_op jit(solution)/shard_map/ppermute | solution.py:37
  52.5 28.5 %collective-permute-start.5 = (bf16[2,128,1024]{2,1,0:T(8,128)(2,1)S(1)}, bf16[2,128,1024]{2,1,0:T(8,128)(2,1)}, u32[]{:S(2)}, u32[]{:S(2)}) collective-permute-start(bf16[2,128,1024]{2,1,0:T(8,128)(2,1)S(1)} %collective-permute-done.4.r1), channel_id=1, source_target_pairs={{1,0},{2,1},{3,2},{32,3},{33,32},{34,33},{35,34},{64,35},{65,64},{... | collective-permute-start | bytes 1572872 | tf_op jit(solution)/shard_map/ppermute | solution.py:37
  223.3 6.6 %collective-permute-start.34 = (bf16[128,1024]{1,0:T(8,128)(2,1)}, bf16[128,1024]{1,0:T(8,128)(2,1)}, u32[]{:S(2)}, u32[]{:S(2)}) collective-permute-start(bf16[128,1024]{1,0:T(8,128)(2,1)} %tie.7.refs_13_), channel_id=1, source_target_pairs={{28,24},{29,25},{30,26},{31,27},{60,56},{61,57},{62,58},{63,59},{9... | collective-permute-start | bytes 786440 | tf_op jit(solution)/shard_map/ppermute | solution.py:48
  243.8 6.4 collective-permute-start.40
  254.0 6.6 %collective-permute-start.43 = (bf16[128,1024]{1,0:T(8,128)(2,1)}, bf16[128,1024]{1,0:T(8,128)(2,1)}, u32[]{:S(2)}, u32[]{:S(2)}) collective-permute-start(bf16[128,1024]{1,0:T(8,128)(2,1)} %tie.10.refs_13_), channel_id=1, source_target_pairs={{16,12},{17,13},{18,14},{19,15},{48,44},{49,45},{50,46},{51,47},{8... | collective-permute-start | bytes 786440 | tf_op jit(solution)/shard_map/ppermute | solution.py:48
  274.5 7.6 %collective-permute-start.49 = (bf16[128,1024]{1,0:T(8,128)(2,1)}, bf16[128,1024]{1,0:T(8,128)(2,1)}, u32[]{:S(2)}, u32[]{:S(2)}) collective-permute-start(bf16[128,1024]{1,0:T(8,128)(2,1)} %tie.12.refs_13_), channel_id=1, source_target_pairs={{8,4},{9,5},{10,6},{11,7},{40,36},{41,37},{42,38},{43,39},{72,68},... | collective-permute-start | bytes 786440 | tf_op jit(solution)/shard_map/ppermute | solution.py:48
  275.9 7.5 %collective-permute-start.50 = (bf16[128,1024]{1,0:T(8,128)(2,1)}, bf16[128,1024]{1,0:T(8,128)(2,1)S(1)}, u32[]{:S(2)}, u32[]{:S(2)}) collective-permute-start(bf16[128,1024]{1,0:T(8,128)(2,1)} %tie.12.refs_13_), channel_id=1, source_target_pairs={{9,4},{10,5},{11,6},{40,7},{41,36},{42,37},{43,38},{72,39},{73,68}... | collective-permute-start | bytes 786440 | tf_op jit(solution)/shard_map/ppermute | solution.py:48
  276.6 6.9 %collective-permute-start.51 = (bf16[128,1024]{1,0:T(8,128)(2,1)}, bf16[128,1024]{1,0:T(8,128)(2,1)S(1)}, u32[]{:S(2)}, u32[]{:S(2)}) collective-permute-start(bf16[128,1024]{1,0:T(8,128)(2,1)} %tie.12.refs_13_), channel_id=1, source_target_pairs={{10,4},{11,5},{40,6},{41,7},{42,36},{43,37},{72,38},{73,39},{74,68... | collective-permute-start | bytes 786440 | tf_op jit(solution)/shard_map/ppermute | solution.py:48
  279.5 121.9 %collective-permute-start.31 = (bf16[128,1024]{1,0:T(8,128)(2,1)S(1)}, bf16[128,1024]{1,0:T(8,128)(2,1)S(1)}, u32[]{:S(2)}, u32[]{:S(2)}) collective-permute-start(bf16[128,1024]{1,0:T(8,128)(2,1)S(1)} %get-tuple-element.149.refs_13_), channel_id=1, source_target_pairs={{4,0},{5,1},{6,2},{7,3},{36,32},{37,33},{38,34},{39,35},{68,64},{6... | collective-permute-start | bytes 786440 | tf_op jit(solution)/shard_map/ppermute | solution.py:48
  280.8 127.4 %collective-permute-start.32 = (bf16[128,1024]{1,0:T(8,128)(2,1)S(1)}, bf16[128,1024]{1,0:T(8,128)(2,1)S(1)}, u32[]{:S(2)}, u32[]{:S(2)}) collective-permute-start(bf16[128,1024]{1,0:T(8,128)(2,1)S(1)} %get-tuple-element.149.refs_13_), channel_id=1, source_target_pairs={{5,0},{6,1},{7,2},{36,3},{37,32},{38,33},{39,34},{68,35},{69,64},{... | collective-permute-start | bytes 786440 | tf_op jit(solution)/shard_map/ppermute | solution.py:48
  282.1 126.5 %collective-permute-start.33 = (bf16[128,1024]{1,0:T(8,128)(2,1)S(1)}, bf16[128,1024]{1,0:T(8,128)(2,1)S(1)}, u32[]{:S(2)}, u32[]{:S(2)}) collective-permute-start(bf16[128,1024]{1,0:T(8,128)(2,1)S(1)} %get-tuple-element.149.refs_13_), channel_id=1, source_target_pairs={{6,0},{7,1},{36,2},{37,3},{38,32},{39,33},{68,34},{69,35},{70,64},... | collective-permute-start | bytes 786440 | tf_op jit(solution)/shard_map/ppermute | solution.py:48
  409.7 15.8 %collective-permute-start.52 = (bf16[128,1024]{1,0:T(8,128)(2,1)}, bf16[128,1024]{1,0:T(8,128)(2,1)S(1)}, u32[]{:S(2)}, u32[]{:S(2)}) collective-permute-start(bf16[128,1024]{1,0:T(8,128)(2,1)} %tie.13.refs_13_), channel_id=1, source_target_pairs={{4,0},{5,1},{6,2},{7,3},{36,32},{37,33},{38,34},{39,35},{68,64},{6... | collective-permute-start | bytes 786440 | tf_op jit(solution)/shard_map/ppermute | solution.py:48
  410.9 14.5 %collective-permute-start.53 = (bf16[128,1024]{1,0:T(8,128)(2,1)}, bf16[128,1024]{1,0:T(8,128)(2,1)}, u32[]{:S(2)}, u32[]{:S(2)}) collective-permute-start(bf16[128,1024]{1,0:T(8,128)(2,1)} %tie.13.refs_13_), channel_id=1, source_target_pairs={{5,0},{6,1},{7,2},{36,3},{37,32},{38,33},{39,34},{68,35},{69,64},{... | collective-permute-start | bytes 786440 | tf_op jit(solution)/shard_map/ppermute | solution.py:48
  412.2 15.3 %collective-permute-start.54 = (bf16[128,1024]{1,0:T(8,128)(2,1)}, bf16[128,1024]{1,0:T(8,128)(2,1)}, u32[]{:S(2)}, u32[]{:S(2)}) collective-permute-start(bf16[128,1024]{1,0:T(8,128)(2,1)} %tie.13.refs_13_), channel_id=1, source_target_pairs={{6,0},{7,1},{36,2},{37,3},{38,32},{39,33},{68,34},{69,35},{70,64},... | collective-permute-start | bytes 786440 | tf_op jit(solution)/shard_map/ppermute | solution.py:48
  444.4 28.6 %collective-permute-start.55 = (f32[1,1024]{1,0:T(1,128)S(1)}, f32[1,1024]{1,0:T(1,128)S(1)}, u32[]{:S(2)}, u32[]{:S(2)}) collective-permute-start(f32[1,1024]{1,0:T(1,128)S(1)} %convert_convert_fusion), channel_id=1, source_target_pairs={{0,128},{1,129},{2,130},{3,131},{32,160},{33,161},{34,162},{35,163... | collective-permute-start | bytes 12296 | tf_op jit(solution)/shard_map/ppermute | solution.py:68
  (101 other events, 527.2 us)
Sparse Core Ops, SparseCore 0:
  9.8 175.8 all-gather.2
  444.5 202.8 reduce-scatter.1

commit v3 on v1

--- a/solution.py
+++ b/solution.py
@@ -70,8 +70,52 @@
 
 def group_sum(value):
     for axis, size in enumerate(group_dims()):
-        value = sum([turn(value, axis, steps) for steps in range(1, size)], value)
+        moving = value
+        for _ in range(size - 1):
+            moving = turn(moving, axis, 1)
+            value = value + moving
     return value
+
+
+def tie_kernel(*refs):
+    del refs
+
+
+def tie(value, *others):
+    anywhere = pl.BlockSpec(memory_space=pl.ANY)
+    return pl.pallas_call(
+        tie_kernel,
+        in_specs=[anywhere] * (1 + len(others)),
+        out_specs=anywhere,
+        out_shape=jax.ShapeDtypeStruct(value.shape, value.dtype),
+        input_output_aliases={0: 0},
+        name="tie",
+    )(value, *others)
+
+
+def ring(value, axis):
+    size, rows = group_dims()[axis], value.shape[0]
+    pieces = [(0, 0, value)]
+    if size == 2:
+        pieces.append((1, 0, turn(value, axis, 1)))
+    if size == 4:
+        half = rows // 2
+        behind, ahead = turn(value, axis, 1), turn(value, axis, -1)
+        pieces.append((1, 0, ahead))
+        pieces.append((2, 0, turn(behind[:half], axis, 1)))
+        pieces.append((2, half, turn(ahead[half:], axis, -1)))
+        pieces.append((3, 0, behind))
+    return pieces
+
+
+def gather_weights(shard):
+    pair = ring(shard[None], 0)
+    firsts = []
+    for part, axis in zip((slice(0, 2), slice(2, 4)), (1, 2)):
+        value = jnp.concatenate([piece[:, part] for _, _, piece in pair])
+        firsts.append(jnp.concatenate([piece for _, _, piece in ring(value, axis)]))
+    firsts = [tie(firsts[0], firsts[1]), tie(firsts[1], firsts[0])]
+    return [ring(first, axis) for first, axis in zip(firsts, (2, 1))]
 
 
 def normed(x, gain):
@@ -80,19 +124,66 @@
     return (as_float * rscale * gain).astype(jnp.bfloat16)
 
 
-def forward_kernel(
-    l2, l1, own, r1, r2, w, gain, seg_col, seg_row,
-    h_out, q_out, k_out, v_out, p_out, pt_out, o_out, a_out,
-    h5, q3, k5, v5,
-):
+def forward_kernel(layout, dims, *refs):
+    count = sum(len(pieces) for pieces in layout)
+    spot, pieces, refs = refs[0], refs[1 : 1 + count], refs[1 + count :]
+    l2, l1, own, r1, r2, gain, seg_col, seg_row = refs[:8]
+    w_out, h_out, q_out, k_out, v_out, p_out, pt_out, o_out, a_out = refs[8:17]
+    w, h5, q3, k5, v5, sems = refs[17:]
+    step = pl.program_id(0)
+    planes, size_y, size_x = dims
+    z, y, x = spot[0], spot[1], spot[2]
+
+    def loads(pair):
+        copies, offset = [], sum(len(pieces) for pieces in layout[:pair])
+        for at, (place, first, rows) in enumerate(layout[pair]):
+            for row in range(rows):
+                one, plane = divmod(first + row, planes)
+                ahead_y, ahead_x = (one, place) if pair == 0 else (place, one)
+                to = lax.rem(z + plane, planes) * size_y + lax.rem(y + ahead_y, size_y)
+                to = to * size_x + lax.rem(x + ahead_x, size_x)
+                share = WIDTH // (planes * size_y * size_x)
+                target = w.at[pl.ds(2 * pair, 2), pl.ds(pl.multiple_of(to * share, share), share), :]
+                copies.append(
+                    pltpu.make_async_copy(
+                        pieces[offset + at].at[row], target, sems.at[pair, len(copies)]
+                    )
+                )
+        return copies
+
+    def store(pair):
+        half = pl.ds(2 * pair, 2)
+        return pltpu.make_async_copy(w.at[half], w_out.at[half], sems.at[2, pair])
+
+    @pl.when(step == 0)
+    def _():
+        for copy in loads(0) + loads(1):
+            copy.start()
+
     gain_row = gain[0:1, :]
     for at, part in enumerate((l2, l1, own, r1, r2)):
         h5[at * BLOCK : (at + 1) * BLOCK, :] = normed(part[0], gain_row)
     h_out[0] = h5[2 * BLOCK : 3 * BLOCK, :]
+
+    @pl.when(step == 0)
+    def _():
+        for copy in loads(0):
+            copy.wait()
+        store(0).start()
+
     for n in range(0, WIDTH, 256):
         cols = slice(n, n + 256)
         q3[:, cols] = dot(h5[2 * BLOCK :, :], w[0, :, cols]).astype(jnp.bfloat16)
         k5[:, cols] = dot(h5[...], w[1, :, cols]).astype(jnp.bfloat16)
+
+    @pl.when(step == 0)
+    def _():
+        for copy in loads(1):
+            copy.wait()
+        store(1).start()
+
+    for n in range(0, WIDTH, 256):
+        cols = slice(n, n + 256)
         v5[:, cols] = dot(h5[...], w[2, :, cols]).astype(jnp.bfloat16)
     q_out[0] = q3[...]
     k_out[0] = k5[: 3 * BLOCK, :]
@@ -103,10 +194,10 @@
             rows = slice(j * BLOCK, (j + 1) * BLOCK)
             keys = slice(j * BLOCK, (j + 3) * BLOCK)
             allowed = seg_col[0, (j + 2) * BLOCK : (j + 3) * BLOCK, 0:1] == seg_row[0, 0:1, keys]
-            score = jnp.where(allowed, dot_nt(q3[rows, cols], k5[keys, cols]) * SCALE, -1e30)
+            score = jnp.where(allowed, dot_nt(q3[rows, cols], k5[keys, cols]), -1e30)
             top = jnp.max(score, axis=-1, keepdims=True)
-            expo = jnp.where(allowed, jnp.exp(score - top), 0.0)
-            p = expo / jnp.sum(expo, axis=-1, keepdims=True)
+            expo = jnp.exp((score - top) * SCALE)
+            p = expo * (1.0 / jnp.sum(expo, axis=-1, keepdims=True))
             high = p.astype(jnp.bfloat16)
             low = (p - high.astype(jnp.float32)).astype(jnp.bfloat16)
             values = v5[keys, cols]
@@ -117,8 +208,19 @@
                 a_out[0, :, cols] = mixed.astype(jnp.bfloat16)
             pt_out[0, head, :, rows] = p[:, (2 - j) * BLOCK : (3 - j) * BLOCK].T
 
-
-def forward(parts, w, gain, seg_col, seg_row):
+    @pl.when(step == MICRO - 1)
+    def _():
+        store(0).wait()
+        store(1).wait()
+
+
+def forward(spot, pairs, parts, gain, seg_col, seg_row):
+    anywhere = pl.BlockSpec(memory_space=pl.ANY)
+    pieces = [piece for pair in pairs for _, _, piece in pair]
+    layout = [[(place, first, piece.shape[0]) for place, first, piece in pair] for pair in pairs]
+    dims = group_dims()
+    most = dims[0] * dims[1] * dims[2]
+
     def per_micro(shape):
         return pl.BlockSpec((1,) + shape, lambda m: (m,) + (0,) * len(shape))
 
@@ -136,29 +238,33 @@
         ((BLOCK, WIDTH), jnp.bfloat16),
     ]
     return pl.pallas_call(
-        forward_kernel,
+        partial(forward_kernel, layout, dims),
         grid=(MICRO,),
-        in_specs=[per_micro((BLOCK, WIDTH))] * 5
+        in_specs=[pl.BlockSpec(memory_space=pltpu.SMEM)]
+        + [anywhere] * len(pieces)
+        + [per_micro((BLOCK, WIDTH))] * 5
         + [
-            whole((3, WIDTH, WIDTH)),
             whole((8, WIDTH)),
             per_micro((5 * BLOCK, 1)),
             per_micro((1, 5 * BLOCK)),
         ],
-        out_specs=[per_micro(shape) for shape, _ in outs],
-        out_shape=[jax.ShapeDtypeStruct((MICRO,) + shape, kind) for shape, kind in outs],
+        out_specs=[anywhere] + [per_micro(shape) for shape, _ in outs],
+        out_shape=[jax.ShapeDtypeStruct((4, WIDTH, WIDTH), jnp.bfloat16)]
+        + [jax.ShapeDtypeStruct((MICRO,) + shape, kind) for shape, kind in outs],
         scratch_shapes=[
+            pltpu.VMEM((4, WIDTH, WIDTH), jnp.bfloat16),
             pltpu.VMEM((5 * BLOCK, WIDTH), jnp.bfloat16),
             pltpu.VMEM((3 * BLOCK, WIDTH), jnp.bfloat16),
             pltpu.VMEM((5 * BLOCK, WIDTH), jnp.bfloat16),
             pltpu.VMEM((5 * BLOCK, WIDTH), jnp.bfloat16),
+            pltpu.SemaphoreType.DMA((3, most)),
         ],
         compiler_params=pltpu.CompilerParams(vmem_limit_bytes=VMEM_LIMIT),
         cost_estimate=pl.CostEstimate(
             flops=2 * 2 * 15 * BLOCK * WIDTH * WIDTH, bytes_accessed=28 << 20, transcendentals=0
         ),
         name="forward",
-    )(*parts, w, gain, seg_col, seg_row)
+    )(spot, *pieces, *parts, gain, seg_col, seg_row)
 
 
 def backward_kernel(micro, first, *refs):
@@ -299,7 +405,10 @@
     block = lax.axis_index(GROUP)
     share = gains.shape[1]
 
-    gathered = lax.all_gather(weights[0], GROUP, axis=1, tiled=True)
+    pairs = gather_weights(weights[0])
+    planes, size_y, _ = group_dims()
+    dp = lax.axis_index("dp")
+    spot = jnp.stack([dp // size_y, dp % size_y, lax.axis_index("fsdp")]).astype(jnp.int32)
     spread = lax.dynamic_update_slice(
         jnp.zeros((1, WIDTH), jnp.float32), gains.astype(jnp.float32), (0, block * share)
     )
@@ -312,7 +421,9 @@
     cot = (cotangent, hop(cotangent, source, sections - 1, 1), hop(cotangent, source, sections - 1, 2))
 
     segs = segments(lengths, block)
-    h, q, k, v, p, pt, o, a = forward(parts, gathered, gain, segs[:, :, None], segs[:, None, :])
+    gathered, h, q, k, v, p, pt, o, a = forward(
+        spot, pairs, parts, gain, segs[:, :, None], segs[:, None, :]
+    )
     kept = (q, k, v, p, pt, o)
 
     stash = [None] * MICRO
@@ -320,10 +431,12 @@
     for at in range(sections - 1, -1, -1):
         flag = (section == at).astype(jnp.int32).reshape(1)
         for micro in range(MICRO):
-            stash[micro] = backward(
-                micro, flag, incoming[micro], gathered, kept, x, gain, stash[micro]
+            stash[micro] = list(
+                backward(micro, flag, incoming[micro], gathered, kept, x, gain, stash[micro])
             )
             if at > 0:
+                if micro > 0:
+                    stash[micro][0] = tie(stash[micro][0], *incoming[micro - 1])
                 incoming[micro] = [hop(stash[micro][0], at, at - 1, back) for back in range(3)]
 
     frame, g, dq, dk, dv, gain_part = (

time: 816 us -> 634 us (0.78)
  starting transfers between devices: 407 us -> 116 us
  waiting for transfers between devices: 313 us -> 375 us
  local copies, waits for them, and re-layouts: 5.68 us -> 43.9 us
    ppermute x44, starting transfers between devices: 370 us -> 38.4 us  [hop(): return lax.ppermute(value, EVERY, pairs)]
    ppermute x44, waiting for transfers between devices: 0.12 us -> 136 us  [hop(): return lax.ppermute(value, EVERY, pairs)]
    all_gather x1 -> x0, waiting for transfers between devices: 103 us -> none  [body(): gathered = lax.all_gather(weights[0], GROUP, axis=1, tiled=True)]
    ppermute x14 -> x31, waiting for transfers between devices: 29 us -> 96.5 us  [turn(): return lax.ppermute(value, GROUP, pairs)]
    ppermute x14 -> x31, starting transfers between devices: 21.3 us -> 59.4 us  [turn(): return lax.ppermute(value, GROUP, pairs)]
    unnamed x16 -> x145, local copies, waits for them, and re-layouts: 2.5 us -> 35.2 us
    ppermute x4, waiting for transfers between devices: 22.5 us -> 1.53 us  [shift(): return lax.ppermute(value, GROUP, pairs)]
    reduce_scatter x1, waiting for transfers between devices: 157 us -> 141 us  [body(): lax.psum_scatter(term.astype(jnp.bfloat16), GROUP, scatter_dimension=1, t...]
  transfers between devices with their start and end apart: 64 -> 80, of which waited for: 14 -> 25; matrix products, arithmetic and copies ran while one was open for 1% -> 2% of each run, Pallas kernels for 2% -> 2%
where the time goes in v3:
time: 634 us; the launch traced here: 623 us
  waiting for transfers between devices  375 us (59%)
  starting transfers between devices  116 us (18%)
  Pallas kernels  59.3 us (9%)
  local copies, waits for them, and re-layouts  43.9 us (7%)
  between operations  15.9 us (3%)
  other arithmetic  10.3 us (2%)
    reduce_scatter x1, waiting for transfers between devices, body(): lax.psum_scatter(term.astype(jnp.bfloat16), GROUP, scatter_dimension=1, t...  141 us
    ppermute x44, waiting for transfers between devices, hop(): return lax.ppermute(value, EVERY, pairs)  136 us
    ppermute x31, waiting for transfers between devices, turn(): return lax.ppermute(value, GROUP, pairs)  96.5 us
    ppermute x31, starting transfers between devices, turn(): return lax.ppermute(value, GROUP, pairs)  59.4 us
    ppermute x44, starting transfers between devices, hop(): return lax.ppermute(value, EVERY, pairs)  38.4 us
    pallas_call x1, Pallas kernels, forward(): pl.pallas_call(partial(forward_kernel, layout, dims), grid=(MICRO,), in_s...  35.6 us
    unnamed x145, local copies, waits for them, and re-layouts  35.2 us
    pallas_call x16, Pallas kernels, backward(): pl.pallas_call(partial(backward_kernel, micro, first), in_specs=[pl.Block...  23.7 us
  transfers between devices with their start and end apart: 80, of which 25 were waited for; matrix products, arithmetic and copies ran while one was open for 2% of the time, Pallas kernels for 2%

profile of v3, /device:TPU:32, one launch (start us, length us, event | category | flops | bytes accessed | tf_op | source)
XLA Modules:
  0.0 623.4 jit_solution(8245144455900518988)
XLA Ops:
  10.2 5.4 collective-permute-done.2
  33.5 11.2 %collective-permute-done.5 = bf16[1,2,32,1024]{3,2,1,0:T(8,128)(2,1)S(1)} collective-permute-done((bf16[1,2,32,1024]{3,2,1,0:T(8,128)(2,1)S(1)}, bf16[1,2,32,1024]{3,2,1,0:T(8,128)(2,1)S(1)}, u32[]{:S(2)}, u32[]{:S(2)}) %collective-permute-start.5) | collective-permute-done | bytes 131104 | tf_op jit(solution)/shard_map/ppermute | solution.py:68
  44.8 6.3 %collective-permute-done.10 = bf16[1,2,32,1024]{3,2,1,0:T(8,128)(2,1)S(1)} collective-permute-done((bf16[1,2,32,1024]{3,2,1,0:T(8,128)(2,1)S(1)}, bf16[1,2,32,1024]{3,2,1,0:T(8,128)(2,1)S(1)}, u32[]{:S(2)}, u32[]{:S(2)}) %collective-permute-start.10) | collective-permute-done | bytes 131104 | tf_op jit(solution)/shard_map/ppermute | solution.py:68
  56.8 4.8 collective-permute-done.24
  61.6 4.8 collective-permute-done.25
  66.6 4.8 collective-permute-done.26
  71.5 4.8 collective-permute-done.27
  92.7 17.6 %collective-permute-done.16.refs_10_ = bf16[8,2,32,1024]{3,2,1,0:T(8,128)(2,1)} collective-permute-done((bf16[8,2,32,1024]{3,2,1,0:T(8,128)(2,1)S(1)}, bf16[8,2,32,1024]{3,2,1,0:T(8,128)(2,1)}, u32[]{:S(2)}, u32[]{:S(2)}) %collective-permute-start.16) | collective-permute-done | bytes 1048608 | tf_op jit(solution)/shard_map/ppermute | solution.py:68
  113.7 10.4 %collective-permute-start.22 = (bf16[2,128,1024]{2,1,0:T(8,128)(2,1)}, bf16[2,128,1024]{2,1,0:T(8,128)(2,1)S(1)}, u32[]{:S(2)}, u32[]{:S(2)}) collective-permute-start(bf16[2,128,1024]{2,1,0:T(8,128)(2,1)} %collective-permute-done.21.refs_14_), channel_id=1, source_target_pairs={{1,0},{2,1},{3,2},{32,3},{33,32},{34,33},{35,34},{64,35},{65,64},{... | collective-permute-start | bytes 1572872 | tf_op jit(solution)/shard_map/ppermute | solution.py:37
  128.5 3.6 collective-permute-start.18
  140.1 35.6 %forward.1 = (bf16[4,1024,1024]{2,1,0:T(8,128)(2,1)}, bf16[2,128,1024]{2,1,0:T(8,128)(2,1)S(1)}, bf16[2,384,1024]{2,1,0:T(8,128)(2,1)}, bf16[2,384,1024]{2,1,0:T...) custom-call(s32[3]{0:T(128)S(1)} %pad_add_fusion.refs_0_, ...), custom_call_target="tpu_custom_call" | custom-call | flops 8053063680 | bytes 29360128 | tf_op jit(solution)/shard_map/forward/pallas_call | solution.py:240
  242.1 130.2 %collective-permute-done.48.refs_1_ = bf16[128,1024]{1,0:T(8,128)(2,1)S(1)} collective-permute-done((bf16[128,1024]{1,0:T(8,128)(2,1)S(1)}, bf16[128,1024]{1,0:T(8,128)(2,1)S(1)}, u32[]{:S(2)}, u32[]{:S(2)}) %collective-permute-start.48) | collective-permute-done | bytes 262176 | tf_op jit(solution)/shard_map/ppermute | solution.py:48
  372.3 4.6 collective-permute-done.49.refs_2_
  384.2 9.8 %backward.23 = (bf16[128,1024]{1,0:T(8,128)(2,1)S(1)}, bf16[128,1024]{1,0:T(8,128)(2,1)S(1)}, bf16[128,1024]{1,0:T(8,128)(2,1)S(1)}, bf16[128,1024]{1,0:T(8,128)...) custom-call(s32[1]{0:T(128)} %bitcast.refs_0_, ...), custom_call_target="tpu_custom_call", output_to_operand_aliasing={{0}: (13, {}), {1}: (14, {}), {2}: (15, {}), {3}: (16, {}),... | custom-call | flops 1879048192 | bytes 16777216 | tf_op jit(solution)/shard_map/backward/pallas_call | solution.py:379
  395.1 9.9 %backward.31 = (bf16[128,1024]{1,0:T(8,128)(2,1)S(1)}, bf16[128,1024]{1,0:T(8,128)(2,1)S(1)}, bf16[128,1024]{1,0:T(8,128)(2,1)S(1)}, bf16[128,1024]{1,0:T(8,128)...) custom-call(s32[1]{0:T(128)} %bitcast.refs_0_, ...), custom_call_target="tpu_custom_call", output_to_operand_aliasing={{0}: (13, {}), {1}: (14, {}), {2}: (15, {}), {3}: (16, {}),... | custom-call | flops 1879048192 | bytes 16777216 | tf_op jit(solution)/shard_map/backward/pallas_call | solution.py:379
  408.1 4.0 pad_maximum_fusion
  412.1 30.0 %collective-permute-start.72 = (f32[1,1024]{1,0:T(1,128)S(1)}, f32[1,1024]{1,0:T(1,128)S(1)}, u32[]{:S(2)}, u32[]{:S(2)}) collective-permute-start(f32[1,1024]{1,0:T(1,128)S(1)} %convert_convert_fusion), channel_id=1, source_target_pairs={{0,128},{1,129},{2,130},{3,131},{32,160},{33,161},{34,162},{35,163... | collective-permute-start | bytes 12296 | tf_op jit(solution)/shard_map/ppermute | solution.py:68
  443.8 4.8 collective-permute-done.73
  448.6 4.9 collective-permute-done.74
  453.4 4.8 collective-permute-done.75
  459.7 3.4 collective-permute-done.76
  463.3 4.6 collective-permute-done.77
  468.8 4.0 collective-permute-done.78
  473.4 140.9 %reduce-scatter.2.cloned.1.call-done = bf16[4,32,1024]{2,1,0:T(8,128)(2,1)} async-done(((bf16[4,1024,1024]{2,1,0:T(8,128)(2,1)}), bf16[4,32,1024]{2,1,0:T(8,128)(2,1)}) %reduce-scatter.2.cloned.1.call-update) | async-done | bytes 262160 | tf_op jit(solution)/shard_map/reduce_scatter | solution.py:454
  (353 shorter events, 142.1 us)
Async XLA Ops:
  7.2 607.1 %reduce-scatter.2.cloned.1.call-start = ((), (), s32[]{:S(2)}) async-start(), calls=%async_computation.1 | async-start | bytes 8650752 | tf_op jit(solution)/shard_map/reduce_scatter | solution.py:454
  23.7 32.8 %collective-permute-start.23 = (f32[1,1024]{1,0:T(1,128)S(1)}, f32[1,1024]{1,0:T(1,128)S(1)}, u32[]{:S(2)}, u32[]{:S(2)}) collective-permute-start(f32[1,1024]{1,0:T(1,128)S(1)} %dynamic_update_slice.5), channel_id=1, source_target_pairs={{0,128},{1,129},{2,130},{3,131},{32,160},{33,161},{34,162},{35,163... | collective-permute-start | bytes 12296 | tf_op jit(solution)/shard_map/ppermute | solution.py:68
  25.0 58.3 %collective-permute-start.19 = (bf16[2,128,1024]{2,1,0:T(8,128)(2,1)}, bf16[2,128,1024]{2,1,0:T(8,128)(2,1)}, u32[]{:S(2)}, u32[]{:S(2)}) collective-permute-start(bf16[2,128,1024]{2,1,0:T(8,128)(2,1)} %bitcast.53), channel_id=1, source_target_pairs={{0,1},{1,2},{2,3},{3,32},{32,33},{33,34},{34,35},{35,64},{64,65},{... | collective-permute-start | bytes 1572872 | tf_op jit(solution)/shard_map/ppermute | solution.py:37
  28.4 16.3 %collective-permute-start.5 = (bf16[1,2,32,1024]{3,2,1,0:T(8,128)(2,1)S(1)}, bf16[1,2,32,1024]{3,2,1,0:T(8,128)(2,1)S(1)}, u32[]{:S(2)}, u32[]{:S(2)}) collective-permute-start(bf16[1,2,32,1024]{3,2,1,0:T(8,128)(2,1)S(1)} %slice.83), channel_id=1, source_target_pairs={{0,32},{1,33},{2,34},{3,35},{32,64},{33,65},{34,66},{35,67},{64,96... | collective-permute-start | bytes 393224 | tf_op jit(solution)/shard_map/ppermute | solution.py:68
  28.9 15.8 %collective-permute-start.6 = (bf16[1,2,32,1024]{3,2,1,0:T(8,128)(2,1)S(1)}, bf16[1,2,32,1024]{3,2,1,0:T(8,128)(2,1)S(1)}, u32[]{:S(2)}, u32[]{:S(2)}) collective-permute-start(bf16[1,2,32,1024]{3,2,1,0:T(8,128)(2,1)S(1)} %slice.84), channel_id=1, source_target_pairs={{0,96},{1,97},{2,98},{3,99},{32,0},{33,1},{34,2},{35,3},{64,32},{6... | collective-permute-start | bytes 393224 | tf_op jit(solution)/shard_map/ppermute | solution.py:68
  31.9 12.8 %collective-permute-start.9 = (bf16[1,2,32,1024]{3,2,1,0:T(8,128)(2,1)S(1)}, bf16[1,2,32,1024]{3,2,1,0:T(8,128)(2,1)S(1)}, u32[]{:S(2)}, u32[]{:S(2)}) collective-permute-start(bf16[1,2,32,1024]{3,2,1,0:T(8,128)(2,1)S(1)} %slice.86), channel_id=1, source_target_pairs={{0,1},{1,2},{2,3},{3,0},{32,33},{33,34},{34,35},{35,32},{64,65},{6... | collective-permute-start | bytes 393224 | tf_op jit(solution)/shard_map/ppermute | solution.py:68
  53.2 35.0 %collective-permute-start.12 = (bf16[8,2,32,1024]{3,2,1,0:T(8,128)(2,1)}, bf16[8,2,32,1024]{3,2,1,0:T(8,128)(2,1)}, u32[]{:S(2)}, u32[]{:S(2)}) collective-permute-start(bf16[8,2,32,1024]{3,2,1,0:T(8,128)(2,1)} %tie.9.refs_1_), channel_id=1, source_target_pairs={{0,1},{1,2},{2,3},{3,0},{32,33},{33,34},{34,35},{35,32},{64,65},{6... | collective-permute-start | bytes 3145736 | tf_op jit(solution)/shard_map/ppermute | solution.py:68
  53.3 36.4 %collective-permute-start.11 = (bf16[8,2,32,1024]{3,2,1,0:T(8,128)(2,1)}, bf16[8,2,32,1024]{3,2,1,0:T(8,128)(2,1)}, u32[]{:S(2)}, u32[]{:S(2)}) collective-permute-start(bf16[8,2,32,1024]{3,2,1,0:T(8,128)(2,1)} %tie.9.refs_1_), channel_id=1, source_target_pairs={{0,3},{1,0},{2,1},{3,2},{32,35},{33,32},{34,33},{35,34},{64,67},{6... | collective-permute-start | bytes 3145736 | tf_op jit(solution)/shard_map/ppermute | solution.py:68
  76.3 11.2 %collective-permute-start.21 = (bf16[2,128,1024]{2,1,0:T(8,128)(2,1)S(1)}, bf16[2,128,1024]{2,1,0:T(8,128)(2,1)}, u32[]{:S(2)}, u32[]{:S(2)}) collective-permute-start(bf16[2,128,1024]{2,1,0:T(8,128)(2,1)S(1)} %bitcast.71), channel_id=1, source_target_pairs={{1,0},{2,1},{3,2},{32,3},{33,32},{34,33},{35,34},{64,35},{65,64},{... | collective-permute-start | bytes 1572872 | tf_op jit(solution)/shard_map/ppermute | solution.py:37
  81.1 29.2 %collective-permute-start.16 = (bf16[8,2,32,1024]{3,2,1,0:T(8,128)(2,1)S(1)}, bf16[8,2,32,1024]{3,2,1,0:T(8,128)(2,1)}, u32[]{:S(2)}, u32[]{:S(2)}) collective-permute-start(bf16[8,2,32,1024]{3,2,1,0:T(8,128)(2,1)S(1)} %copy-done.48), channel_id=1, source_target_pairs={{0,32},{1,33},{2,34},{3,35},{32,64},{33,65},{34,66},{35,67},{64,96... | collective-permute-start | bytes 3145736 | tf_op jit(solution)/shard_map/ppermute | solution.py:68
  83.3 30.3 %collective-permute-start.15 = (bf16[8,2,32,1024]{3,2,1,0:T(8,128)(2,1)S(1)}, bf16[8,2,32,1024]{3,2,1,0:T(8,128)(2,1)}, u32[]{:S(2)}, u32[]{:S(2)}) collective-permute-start(bf16[8,2,32,1024]{3,2,1,0:T(8,128)(2,1)S(1)} %copy-done.48), channel_id=1, source_target_pairs={{0,96},{1,97},{2,98},{3,99},{32,0},{33,1},{34,2},{35,3},{64,32},{6... | collective-permute-start | bytes 3145736 | tf_op jit(solution)/shard_map/ppermute | solution.py:68
  87.5 37.7 %collective-permute-start.1 = (bf16[2,128,1024]{2,1,0:T(8,128)(2,1)S(1)}, bf16[2,128,1024]{2,1,0:T(8,128)(2,1)S(1)}, u32[]{:S(2)}, u32[]{:S(2)}) collective-permute-start(bf16[2,128,1024]{2,1,0:T(8,128)(2,1)S(1)} %copy-done.56), channel_id=1, source_target_pairs={{22,28},{23,29},{52,30},{53,31},{54,60},{55,61},{84,62},{85,63},{8... | collective-permute-start | bytes 1572872 | tf_op jit(solution)/shard_map/ppermute | solution.py:48
  88.2 40.3 %collective-permute-start = (bf16[2,128,1024]{2,1,0:T(8,128)(2,1)S(1)}, bf16[2,128,1024]{2,1,0:T(8,128)(2,1)}, u32[]{:S(2)}, u32[]{:S(2)}) collective-permute-start(bf16[2,128,1024]{2,1,0:T(8,128)(2,1)S(1)} %copy-done.56), channel_id=1, source_target_pairs={{21,28},{22,29},{23,30},{52,31},{53,60},{54,61},{55,62},{84,63},{8... | collective-permute-start | bytes 1572872 | tf_op jit(solution)/shard_map/ppermute | solution.py:48
  89.7 38.8 %collective-permute-start.20 = (bf16[2,128,1024]{2,1,0:T(8,128)(2,1)}, bf16[2,128,1024]{2,1,0:T(8,128)(2,1)}, u32[]{:S(2)}, u32[]{:S(2)}) collective-permute-start(bf16[2,128,1024]{2,1,0:T(8,128)(2,1)} %collective-permute-done.19.refs_12_), channel_id=1, source_target_pairs={{0,1},{1,2},{2,3},{3,32},{32,33},{33,34},{34,35},{35,64},{64,65},{... | collective-permute-start | bytes 1572872 | tf_op jit(solution)/shard_map/ppermute | solution.py:37
  110.3 14.8 %collective-permute-start.29 = (f32[1,1024]{1,0:T(1,128)S(1)}, f32[1,1024]{1,0:T(1,128)S(1)}, u32[]{:S(2)}, u32[]{:S(2)}) collective-permute-start(f32[1,1024]{1,0:T(1,128)S(1)} %collective-permute-done.28), channel_id=1, source_target_pairs={{0,1},{1,2},{2,3},{3,0},{32,33},{33,34},{34,35},{35,32},{64,65},{6... | collective-permute-start | bytes 12296 | tf_op jit(solution)/shard_map/ppermute | solution.py:68
  113.7 20.4 %collective-permute-start.22 = (bf16[2,128,1024]{2,1,0:T(8,128)(2,1)}, bf16[2,128,1024]{2,1,0:T(8,128)(2,1)S(1)}, u32[]{:S(2)}, u32[]{:S(2)}) collective-permute-start(bf16[2,128,1024]{2,1,0:T(8,128)(2,1)} %collective-permute-done.21.refs_14_), channel_id=1, source_target_pairs={{1,0},{2,1},{3,2},{32,3},{33,32},{34,33},{35,34},{64,35},{65,64},{... | collective-permute-start | bytes 1572872 | tf_op jit(solution)/shard_map/ppermute | solution.py:37
  125.1 11.3 %collective-permute-start.13 = (bf16[4,2,32,1024]{3,2,1,0:T(8,128)(2,1)S(1)}, bf16[4,2,32,1024]{3,2,1,0:T(8,128)(2,1)S(1)}, u32[]{:S(2)}, u32[]{:S(2)}) collective-permute-start(bf16[4,2,32,1024]{3,2,1,0:T(8,128)(2,1)S(1)} %slice.88), channel_id=1, source_target_pairs={{0,1},{1,2},{2,3},{3,0},{32,33},{33,34},{34,35},{35,32},{64,65},{6... | collective-permute-start | bytes 1572872 | tf_op jit(solution)/shard_map/ppermute | solution.py:68
  236.6 135.7 %collective-permute-start.48 = (bf16[128,1024]{1,0:T(8,128)(2,1)S(1)}, bf16[128,1024]{1,0:T(8,128)(2,1)S(1)}, u32[]{:S(2)}, u32[]{:S(2)}) collective-permute-start(bf16[128,1024]{1,0:T(8,128)(2,1)S(1)} %get-tuple-element.151.refs_13_), channel_id=1, source_target_pairs={{4,0},{5,1},{6,2},{7,3},{36,32},{37,33},{38,34},{39,35},{68,64},{6... | collective-permute-start | bytes 786440 | tf_op jit(solution)/shard_map/ppermute | solution.py:48
  237.9 139.0 %collective-permute-start.49 = (bf16[128,1024]{1,0:T(8,128)(2,1)S(1)}, bf16[128,1024]{1,0:T(8,128)(2,1)S(1)}, u32[]{:S(2)}, u32[]{:S(2)}) collective-permute-start(bf16[128,1024]{1,0:T(8,128)(2,1)S(1)} %get-tuple-element.151.refs_13_), channel_id=1, source_target_pairs={{5,0},{6,1},{7,2},{36,3},{37,32},{38,33},{39,34},{68,35},{69,64},{... | collective-permute-start | bytes 786440 | tf_op jit(solution)/shard_map/ppermute | solution.py:48
  239.2 138.0 %collective-permute-start.50 = (bf16[128,1024]{1,0:T(8,128)(2,1)S(1)}, bf16[128,1024]{1,0:T(8,128)(2,1)S(1)}, u32[]{:S(2)}, u32[]{:S(2)}) collective-permute-start(bf16[128,1024]{1,0:T(8,128)(2,1)S(1)} %get-tuple-element.151.refs_13_), channel_id=1, source_target_pairs={{6,0},{7,1},{36,2},{37,3},{38,32},{39,33},{68,34},{69,35},{70,64},... | collective-permute-start | bytes 786440 | tf_op jit(solution)/shard_map/ppermute | solution.py:48
  378.4 15.6 %collective-permute-start.69 = (bf16[128,1024]{1,0:T(8,128)(2,1)}, bf16[128,1024]{1,0:T(8,128)(2,1)S(1)}, u32[]{:S(2)}, u32[]{:S(2)}) collective-permute-start(bf16[128,1024]{1,0:T(8,128)(2,1)} %tie.17.refs_13_), channel_id=1, source_target_pairs={{4,0},{5,1},{6,2},{7,3},{36,32},{37,33},{38,34},{39,35},{68,64},{6... | collective-permute-start | bytes 786440 | tf_op jit(solution)/shard_map/ppermute | solution.py:48
  379.7 14.3 %collective-permute-start.70 = (bf16[128,1024]{1,0:T(8,128)(2,1)}, bf16[128,1024]{1,0:T(8,128)(2,1)}, u32[]{:S(2)}, u32[]{:S(2)}) collective-permute-start(bf16[128,1024]{1,0:T(8,128)(2,1)} %tie.17.refs_13_), channel_id=1, source_target_pairs={{5,0},{6,1},{7,2},{36,3},{37,32},{38,33},{39,34},{68,35},{69,64},{... | collective-permute-start | bytes 786440 | tf_op jit(solution)/shard_map/ppermute | solution.py:48
  381.0 14.2 %collective-permute-start.71 = (bf16[128,1024]{1,0:T(8,128)(2,1)}, bf16[128,1024]{1,0:T(8,128)(2,1)}, u32[]{:S(2)}, u32[]{:S(2)}) collective-permute-start(bf16[128,1024]{1,0:T(8,128)(2,1)} %tie.17.refs_13_), channel_id=1, source_target_pairs={{6,0},{7,1},{36,2},{37,3},{38,32},{39,33},{68,34},{69,35},{70,64},... | collective-permute-start | bytes 786440 | tf_op jit(solution)/shard_map/ppermute | solution.py:48
  412.1 31.6 %collective-permute-start.72 = (f32[1,1024]{1,0:T(1,128)S(1)}, f32[1,1024]{1,0:T(1,128)S(1)}, u32[]{:S(2)}, u32[]{:S(2)}) collective-permute-start(f32[1,1024]{1,0:T(1,128)S(1)} %convert_convert_fusion), channel_id=1, source_target_pairs={{0,128},{1,129},{2,130},{3,131},{32,160},{33,161},{34,162},{35,163... | collective-permute-start | bytes 12296 | tf_op jit(solution)/shard_map/ppermute | solution.py:68
  (125 other events, 516.4 us)
Sparse Core Ops, SparseCore 0:
  412.2 201.9 reduce-scatter.1

commit v4 on v3

--- a/solution.py
+++ b/solution.py
@@ -66,15 +66,6 @@
                 index = lambda p: (p[0] * dims[1] + p[1]) * dims[2] + p[2]
                 pairs.append((index(at), index(to)))
     return lax.ppermute(value, GROUP, pairs)
-
-
-def group_sum(value):
-    for axis, size in enumerate(group_dims()):
-        moving = value
-        for _ in range(size - 1):
-            moving = turn(moving, axis, 1)
-            value = value + moving
-    return value
 
 
 def tie_kernel(*refs):
@@ -267,9 +258,9 @@
     )(spot, *pieces, *parts, gain, seg_col, seg_row)
 
 
-def backward_kernel(micro, first, *refs):
+def backward_kernel(micro, *refs):
     flag, g0, g1, g2, w, q_in, k_in, v_in, p_in, pt_in, o_in, x_in, gain_in = refs[:13]
-    refs = refs[13 if first else 19 :]
+    refs = refs[13:]
     frame_out, g_out, dq_out, dk_out, dv_out, gain_out = refs[:6]
     g, wv, q, k, v, p, pt, o, x, gain, da, dq, dk, dv, dh, frame, gain_sum, sems = refs[6:]
 
@@ -350,12 +341,12 @@
             copy.wait()
 
 
-def backward(micro, flag, incoming, w, kept, x, gain, stash):
+def backward(micro, flag, incoming, w, kept, x, gain):
     block = jax.ShapeDtypeStruct((BLOCK, WIDTH), jnp.bfloat16)
     outs = [block] * 5 + [jax.ShapeDtypeStruct((8, WIDTH), jnp.float32)]
-    first = stash is None
-    operands = [flag, *incoming, w, *kept, x, gain] + ([] if first else list(stash))
+    operands = [flag, *incoming, w, *kept, x, gain]
     anywhere = pl.BlockSpec(memory_space=pl.ANY)
+    in_hbm = pl.BlockSpec(memory_space=pltpu.HBM)
     bf16, f32 = jnp.bfloat16, jnp.float32
     scratch = [
         ((3 * BLOCK, WIDTH), bf16),
@@ -377,13 +368,12 @@
         ((8, WIDTH), f32),
     ]
     return pl.pallas_call(
-        partial(backward_kernel, micro, first),
+        partial(backward_kernel, micro),
         in_specs=[pl.BlockSpec(memory_space=pltpu.SMEM)] + [anywhere] * (len(operands) - 1),
-        out_specs=[anywhere] * 6,
+        out_specs=[in_hbm] * 6,
         out_shape=outs,
         scratch_shapes=[pltpu.VMEM(shape, kind) for shape, kind in scratch]
         + [pltpu.SemaphoreType.DMA((19,))],
-        input_output_aliases={} if first else {13 + at: at for at in range(6)},
         compiler_params=pltpu.CompilerParams(vmem_limit_bytes=VMEM_LIMIT),
         cost_estimate=pl.CostEstimate(
             flops=2 * 7 * BLOCK * WIDTH * WIDTH, bytes_accessed=16 << 20, transcendentals=0
@@ -392,6 +382,167 @@
     )(*operands)
 
 
+def ring_slots(size):
+    if size == 4:
+        return (2, 2, 2, 1, 1), {
+            (0, 0): (0, 0), (1, 0): (0, 1),
+            (0, 1): (3, 0), (1, 1): (1, 1),
+            (0, 2): (1, 0), (1, 2): (2, 1),
+            (0, 3): (2, 0), (1, 3): (4, 0),
+        }
+    return (2,) * size, {(m, f): (f, m) for m in range(2) for f in range(size)}
+
+
+def add(*values):
+    return sum(value.astype(jnp.float32) for value in values)
+
+
+def ring_sum(parts, axis):
+    size = group_dims()[axis]
+    if size == 4:
+        keep, up, down, late_up, late_down = parts
+        up, down = turn(up, axis, 1), turn(down, axis, -1)
+        late_up = add(late_up[0], up[0]).astype(jnp.bfloat16)
+        late_down = add(late_down[0], down[1]).astype(jnp.bfloat16)
+        late_up, late_down = turn(late_up, axis, 1), turn(late_down, axis, -1)
+        return jnp.stack([add(keep[0], late_up, down[0]), add(keep[1], up[1], late_down)])
+    if size == 2:
+        return add(parts[0], turn(parts[1], axis, 1))
+    return parts[0].astype(jnp.float32)
+
+
+def collect_kernel(sections, dims, counts, *refs):
+    place, spot, h_in, a_in = refs[:4]
+    kept = refs[4 : 4 + 12 * sections]
+    refs = refs[4 + 12 * sections :]
+    frame_out, gain_out, outs = refs[0], refs[1], refs[2 : 2 + sum(counts)]
+    left, right, term, frame, gain, sems, out_sems = refs[2 + sum(counts) :]
+    planes, size_y, size_x = dims
+    share = WIDTH // (planes * size_y * size_x)
+    own_y, own_x = spot[1], spot[2]
+    names = ("frame", "g", "dq", "dk", "dv", "gain")
+
+    def copies(at):
+        found = []
+        for micro in range(MICRO):
+            results = dict(zip(names, kept[(at * MICRO + micro) * 6 : (at * MICRO + micro + 1) * 6]))
+            rows = pl.ds(micro * BLOCK, BLOCK)
+            pairs = [(results[name], right.at[n, rows]) for n, name in enumerate(("dq", "dk", "dv", "g"))]
+            pairs += [(results["frame"], frame.at[micro]), (results["gain"], gain.at[micro])]
+            pairs += [(h_in.at[micro], left.at[0, rows]), (a_in.at[micro], left.at[1, rows])]
+            found += [
+                pltpu.make_async_copy(source, target, sems.at[micro, n])
+                for n, (source, target) in enumerate(pairs)
+            ]
+        return found
+
+    for at in range(sections):
+
+        @pl.when(place[0] == at)
+        def _(at=at):
+            started = copies(at)
+            for copy in started:
+                copy.start()
+            for copy in started:
+                copy.wait()
+
+    frame_copy = pltpu.make_async_copy(frame, frame_out, out_sems.at[4, 0])
+    frame_copy.start()
+    gain[0] = gain[0] + gain[1]
+    gain_copy = pltpu.make_async_copy(gain.at[0], gain_out, out_sems.at[4, 1])
+    gain_copy.start()
+
+    started = [frame_copy, gain_copy]
+    for m in range(4):
+        pair = m // 2
+        first_size, second_size = (size_x, size_y) if pair == 0 else (size_y, size_x)
+        _, slots = ring_slots(first_size)
+        arrays = outs[: counts[0]] if pair == 0 else outs[counts[0] :]
+        factor = left[1 if m == 3 else 0]
+        for n in range(0, WIDTH, 256):
+            cols = slice(n, n + 256)
+            term[m, :, cols] = dot_tn(factor, right[m, :, cols]).astype(jnp.bfloat16)
+        number = 0
+        for f in range(first_size):
+            array, row = slots[m % 2, f]
+            for r in range(second_size):
+                ahead_x, ahead_y = (f, r) if pair == 0 else (r, f)
+                column = lax.rem(own_y + ahead_y, size_y) * size_x + lax.rem(own_x + ahead_x, size_x)
+                for plane in range(planes):
+                    at = (plane * size_y * size_x + column) * share
+                    copy = pltpu.make_async_copy(
+                        term.at[m, pl.ds(pl.multiple_of(at, share), share), :],
+                        arrays[array].at[row, r, plane],
+                        out_sems.at[m, number],
+                    )
+                    copy.start()
+                    started.append(copy)
+                    number += 1
+    for copy in started:
+        copy.wait()
+
+
+def collect(section, spot, h, a, kept):
+    dims, sections = group_dims(), len(kept)
+    planes, size_y, size_x = dims
+    total = planes * size_y * size_x
+    share = WIDTH // total
+    anywhere = pl.BlockSpec(memory_space=pl.ANY)
+    in_hbm = pl.BlockSpec(memory_space=pltpu.HBM)
+    smem = pl.BlockSpec(memory_space=pltpu.SMEM)
+    shapes, counts = [], []
+    for first_size, second_size in ((size_x, size_y), (size_y, size_x)):
+        rows, _ = ring_slots(first_size)
+        counts.append(len(rows))
+        shapes += [
+            jax.ShapeDtypeStruct((n, second_size, planes, share, WIDTH), jnp.bfloat16) for n in rows
+        ]
+    operands = [result for both in kept for results in both for result in results]
+    outs = pl.pallas_call(
+        partial(collect_kernel, sections, dims, counts),
+        in_specs=[smem, smem] + [anywhere] * (2 + len(operands)),
+        out_specs=[in_hbm] * (2 + len(shapes)),
+        out_shape=[
+            jax.ShapeDtypeStruct((MICRO, BLOCK, WIDTH), jnp.bfloat16),
+            jax.ShapeDtypeStruct((8, WIDTH), jnp.float32),
+        ]
+        + shapes,
+        scratch_shapes=[
+            pltpu.VMEM((2, MICRO * BLOCK, WIDTH), jnp.bfloat16),
+            pltpu.VMEM((4, MICRO * BLOCK, WIDTH), jnp.bfloat16),
+            pltpu.VMEM((4, WIDTH, WIDTH), jnp.bfloat16),
+            pltpu.VMEM((MICRO, BLOCK, WIDTH), jnp.bfloat16),
+            pltpu.VMEM((MICRO, 8, WIDTH), jnp.float32),
+            pltpu.SemaphoreType.DMA((MICRO, 8)),
+            pltpu.SemaphoreType.DMA((5, max(total, 2))),
+        ],
+        compiler_params=pltpu.CompilerParams(vmem_limit_bytes=VMEM_LIMIT),
+        cost_estimate=pl.CostEstimate(
+            flops=2 * 8 * BLOCK * WIDTH * WIDTH, bytes_accessed=14 << 20, transcendentals=0
+        ),
+        name="collect",
+    )(section, spot, h, a, *operands)
+    frame, gain = outs[:2]
+    return frame, gain, [outs[2 : 2 + counts[0]], outs[2 + counts[0] :]]
+
+
+def sum_terms(parts, plane):
+    totals = []
+    for pair, (first, second) in zip(parts, ((2, 1), (1, 2))):
+        value = ring_sum(pair, first).astype(jnp.bfloat16)
+        rows, slots = ring_slots(group_dims()[second])
+        arrays = [[None] * n for n in rows]
+        for (m, f), (array, row) in slots.items():
+            arrays[array][row] = value[m, f]
+        value = ring_sum([jnp.stack(array) for array in arrays], second)
+        totals.append(value)
+    value = jnp.concatenate(totals)
+    if group_dims()[0] == 1:
+        return value[:, 0]
+    other = lax.dynamic_index_in_dim(value, 1 - plane, 1, keepdims=False).astype(jnp.bfloat16)
+    return add(lax.dynamic_index_in_dim(value, plane, 1, keepdims=False), turn(other, 0, 1))
+
+
 def segments(lengths, block):
     bounds = jnp.cumsum(lengths, axis=1)
     total = lax.axis_size(GROUP) * BLOCK
@@ -409,10 +560,9 @@
     planes, size_y, _ = group_dims()
     dp = lax.axis_index("dp")
     spot = jnp.stack([dp // size_y, dp % size_y, lax.axis_index("fsdp")]).astype(jnp.int32)
-    spread = lax.dynamic_update_slice(
-        jnp.zeros((1, WIDTH), jnp.float32), gains.astype(jnp.float32), (0, block * share)
-    )
-    gain = jnp.broadcast_to(group_sum(spread), (8, WIDTH))
+    spread = jnp.zeros((8, max(share, 128)), jnp.float32).at[:1, :share].set(gains.astype(jnp.float32))
+    spread = lax.all_gather(spread, GROUP, axis=0)
+    gain = jnp.broadcast_to(spread[:, 0, :share].reshape(1, WIDTH), (8, WIDTH))
 
     x = checkpoints[0]
     left, right = shift(x, 1), shift(x, -1)
@@ -426,37 +576,26 @@
     )
     kept = (q, k, v, p, pt, o)
 
-    stash = [None] * MICRO
+    kept_grads = [[None] * MICRO for _ in range(sections)]
     incoming = [[part[micro] for part in cot] for micro in range(MICRO)]
     for at in range(sections - 1, -1, -1):
         flag = (section == at).astype(jnp.int32).reshape(1)
         for micro in range(MICRO):
-            stash[micro] = list(
-                backward(micro, flag, incoming[micro], gathered, kept, x, gain, stash[micro])
-            )
+            grads = list(backward(micro, flag, incoming[micro], gathered, kept, x, gain))
             if at > 0:
                 if micro > 0:
-                    stash[micro][0] = tie(stash[micro][0], *incoming[micro - 1])
-                incoming[micro] = [hop(stash[micro][0], at, at - 1, back) for back in range(3)]
-
-    frame, g, dq, dk, dv, gain_part = (
-        [stash[micro][at] for micro in range(MICRO)] for at in range(6)
-    )
-    h, a = h.reshape(-1, WIDTH), a.reshape(-1, WIDTH)
-    term = jnp.stack(
-        [
-            dot_tn(h, jnp.concatenate(dq)),
-            dot_tn(h, jnp.concatenate(dk)),
-            dot_tn(h, jnp.concatenate(dv)),
-            dot_tn(a, jnp.concatenate(g)),
-        ]
-    )
-    weight_part = lax.psum_scatter(
-        term.astype(jnp.bfloat16), GROUP, scatter_dimension=1, tiled=True
-    ).astype(jnp.float32)
-    gain_term = (gain_part[0][0:1] + gain_part[1][0:1]).astype(jnp.bfloat16).astype(jnp.float32)
-    gain_sum = lax.dynamic_slice(group_sum(gain_term), (0, block * share), (1, share))
-    return (jnp.stack(frame)[None], weight_part[None], gain_sum)
+                    grads[0] = tie(grads[0], *incoming[micro - 1])
+                incoming[micro] = [hop(grads[0], at, at - 1, back) for back in range(3)]
+            kept_grads[at][micro] = grads
+
+    place = section.astype(jnp.int32).reshape(1)
+    frame, gain_part, parts = collect(place, spot, h, a, kept_grads)
+    weight_part = sum_terms(parts, spot[0])
+    gain_term = gain_part[0:1].astype(jnp.bfloat16).astype(jnp.float32)
+    gain_term = lax.all_gather(gain_term.reshape(8, WIDTH // 8), GROUP, axis=0)
+    gain_sum = jnp.sum(gain_term, axis=0).reshape(1, WIDTH)
+    gain_sum = lax.dynamic_slice(gain_sum, (0, block * share), (1, share))
+    return (frame[None], weight_part[None], gain_sum)
 
 
 def solution(mesh):

time: 634 us -> 635 us (level)
  waiting for transfers between devices: 375 us -> 190 us
  blocking collectives: 0 us -> 157 us
  local copies, waits for them, and re-layouts: 43.9 us -> 86 us
  between operations: 15.9 us -> 2.94 us
  Pallas kernels: 59.3 us -> 67.3 us
    all_gather x0 -> x2, blocking collectives: none -> 157 us  [the longest x1 78.9 us: body(): spread = lax.all_gather(spread, GROUP, axis=0)]
    reduce_scatter x1 -> x0, waiting for transfers between devices: 141 us -> none  [body(): lax.psum_scatter(term.astype(jnp.bfloat16), GROUP, scatter_dimension=1, t...]
    unnamed x145 -> x267, local copies, waits for them, and re-layouts: 35.2 us -> 74 us
    ppermute x31 -> x34, waiting for transfers between devices: 96.5 us -> 58.8 us  [turn(): return lax.ppermute(value, GROUP, pairs)]
    ppermute x44, waiting for transfers between devices: 136 us -> 113 us  [hop(): return lax.ppermute(value, EVERY, pairs)]
    ppermute x4, waiting for transfers between devices: 1.53 us -> 18.1 us  [shift(): return lax.ppermute(value, GROUP, pairs)]
    pallas_call x16 -> x17, Pallas kernels: 23.7 us -> 31.7 us  [the longest x16 23.6 us: backward(): pl.pallas_call(partial(backward_kernel, micro), in_specs=[pl.BlockSpec(me...]
    ppermute x31 -> x34, starting transfers between devices: 59.4 us -> 58.8 us  [turn(): return lax.ppermute(value, GROUP, pairs)]
  transfers between devices with their start and end apart: 80 -> 82, of which waited for: 25 -> 20; matrix products, arithmetic and copies ran while one was open for 2% -> 3% of each run, Pallas kernels for 2% -> 2%
where the time goes in v4:
time: 635 us; the launch traced here: 625 us
  waiting for transfers between devices  190 us (30%)
  blocking collectives  157 us (25%)
  starting transfers between devices  113 us (18%)
  local copies, waits for them, and re-layouts  86 us (14%)
  Pallas kernels  67.3 us (11%)
  other arithmetic  8.52 us (1%)
    ppermute x44, waiting for transfers between devices, hop(): return lax.ppermute(value, EVERY, pairs)  113 us
    all_gather x1, blocking collectives, body(): spread = lax.all_gather(spread, GROUP, axis=0)  78.9 us
    all_gather x1, blocking collectives, body(): gain_term = lax.all_gather(gain_term.reshape(8, WIDTH // 8), GROUP, axis=0)  78.1 us
    unnamed x267, local copies, waits for them, and re-layouts  74 us
    ppermute x34, waiting for transfers between devices, turn(): return lax.ppermute(value, GROUP, pairs)  58.8 us
    ppermute x34, starting transfers between devices, turn(): return lax.ppermute(value, GROUP, pairs)  58.8 us
    pallas_call x1, Pallas kernels, forward(): pl.pallas_call(partial(forward_kernel, layout, dims), grid=(MICRO,), in_s...  35.6 us
    ppermute x44, starting transfers between devices, hop(): return lax.ppermute(value, EVERY, pairs)  34.1 us
  transfers between devices with their start and end apart: 82, of which 20 were waited for; matrix products, arithmetic and copies ran while one was open for 3% of the time, Pallas kernels for 2%

profile of v4, /device:TPU:32, one launch (start us, length us, event | category | flops | bytes accessed | tf_op | source)
XLA Modules:
  0.0 625.0 jit_solution(5335067601470323585)
XLA Ops:
  3.6 5.4 collective-permute-done
  9.1 3.1 collective-permute-start.1
  15.5 4.8 collective-permute-done.2
  20.4 3.3 collective-permute-start.4
  38.0 7.9 %collective-permute-start.19 = (bf16[2,128,1024]{2,1,0:T(8,128)(2,1)S(1)}, bf16[2,128,1024]{2,1,0:T(8,128)(2,1)}, u32[]{:S(2)}, u32[]{:S(2)}) collective-permute-start(bf16[2,128,1024]{2,1,0:T(8,128)(2,1)S(1)} %bitcast.204), channel_id=1, source_target_pairs={{1,0},{2,1},{3,2},{32,3},{33,32},{34,33},{35,34},{64,35},{65,64},{... | collective-permute-start | bytes 1572872 | tf_op jit(solution)/shard_map/ppermute | solution.py:37
  46.0 18.1 %collective-permute-done.17.refs_12_ = bf16[2,128,1024]{2,1,0:T(8,128)(2,1)} collective-permute-done((bf16[2,128,1024]{2,1,0:T(8,128)(2,1)S(1)}, bf16[2,128,1024]{2,1,0:T(8,128)(2,1)}, u32[]{:S(2)}, u32[]{:S(2)}) %collective-permute-start.17) | collective-permute-done | bytes 524320 | tf_op jit(solution)/shard_map/ppermute | solution.py:37
  65.5 78.9 %all_gather.10 = f32[32,8,128]{2,1,0:T(8,128)S(1)} all-gather(f32[1,8,128]{2,1,0:T(8,128)S(1)} %pad_convert_fusion), channel_id=1, replica_groups=mesh['dp'=8,'section'=8,'fsdp'=4] {'dp','fsdp'}, dimensions={0}, use_global_device_ids=true | all-gather | bytes 135168 | tf_op jit(solution)/shard_map/all_gather | solution.py:564
  154.9 8.1 %collective-permute-start.20 = (bf16[2,128,1024]{2,1,0:T(8,128)(2,1)}, bf16[2,128,1024]{2,1,0:T(8,128)(2,1)}, u32[]{:S(2)}, u32[]{:S(2)}) collective-permute-start(bf16[2,128,1024]{2,1,0:T(8,128)(2,1)} %collective-permute-done.19.refs_14_), channel_id=1, source_target_pairs={{1,0},{2,1},{3,2},{32,3},{33,32},{34,33},{35,34},{64,35},{65,64},{... | collective-permute-start | bytes 1572872 | tf_op jit(solution)/shard_map/ppermute | solution.py:37
  166.2 3.3 collective-permute-start.12
  169.5 3.2 collective-permute-start.16
  176.5 3.7 collective-permute-done.15.refs_8_
  180.3 35.6 %forward.1 = (bf16[4,1024,1024]{2,1,0:T(8,128)(2,1)}, bf16[2,128,1024]{2,1,0:T(8,128)(2,1)S(1)}, bf16[2,384,1024]{2,1,0:T(8,128)(2,1)}, bf16[2,384,1024]{2,1,0:T...) custom-call(s32[3]{0:T(128)S(1)} %pad_add_fusion.refs_0_.refs_1_, ...), custom_call_target="tpu_custom_call" | custom-call | flops 8053063680 | bytes 29360128 | tf_op jit(solution)/shard_map/forward/pallas_call | solution.py:231
  314.4 100.6 %collective-permute-done.41.refs_1_ = bf16[128,1024]{1,0:T(8,128)(2,1)S(1)} collective-permute-done((bf16[128,1024]{1,0:T(8,128)(2,1)S(1)}, bf16[128,1024]{1,0:T(8,128)(2,1)S(1)}, u32[]{:S(2)}, u32[]{:S(2)}) %collective-permute-start.41) | collective-permute-done | bytes 262176 | tf_op jit(solution)/shard_map/ppermute | solution.py:48
  415.0 10.1 %collective-permute-done.42.refs_2_ = bf16[128,1024]{1,0:T(8,128)(2,1)S(1)} collective-permute-done((bf16[128,1024]{1,0:T(8,128)(2,1)S(1)}, bf16[128,1024]{1,0:T(8,128)(2,1)S(1)}, u32[]{:S(2)}, u32[]{:S(2)}) %collective-permute-start.42) | collective-permute-done | bytes 262176 | tf_op jit(solution)/shard_map/ppermute | solution.py:48
  431.7 9.8 %backward.23 = (bf16[128,1024]{1,0:T(8,128)(2,1)S(1)}, bf16[128,1024]{1,0:T(8,128)(2,1)S(1)}, bf16[128,1024]{1,0:T(8,128)(2,1)S(1)}, bf16[128,1024]{1,0:T(8,128)...) custom-call(s32[1]{0:T(128)} %bitcast.7.refs_0_, bf16[128,1024]{1,0:T(8,128)(2,1)S(1)} %copy-done.11, ...), custom_call_target="tpu_custom_call" | custom-call | flops 1879048192 | bytes 16777216 | tf_op jit(solution)/shard_map/backward/pallas_call | solution.py:370
  444.7 9.6 %backward.31 = (bf16[128,1024]{1,0:T(8,128)(2,1)S(1)}, bf16[128,1024]{1,0:T(8,128)(2,1)S(1)}, bf16[128,1024]{1,0:T(8,128)(2,1)S(1)}, bf16[128,1024]{1,0:T(8,128)...) custom-call(s32[1]{0:T(128)} %bitcast.7.refs_0_, bf16[128,1024]{1,0:T(8,128)(2,1)S(1)} %collective-permute-done.62.refs_1_, ...), custom_call_target="tpu_custom_call" | custom-call | flops 1879048192 | bytes 16777216 | tf_op jit(solution)/shard_map/backward/pallas_call | solution.py:370
  457.9 8.1 %collect.1 = (bf16[2,128,1024]{2,1,0:T(8,128)(2,1)}, f32[8,1024]{1,0:T(8,128)S(1)}, bf16[2,4,2,32,1024]{4,3,2,1,0:T(8,128)(2,1)}, bf16[2,4,2,32,1024]{4,3,2,1,0:...) custom-call(s32[1]{0:T(128)} %bitcast.refs_0_, ...), custom_call_target="tpu_custom_call" | custom-call | flops 2147483648 | bytes 14680064 | tf_op jit(solution)/shard_map/collect/pallas_call | solution.py:501
  471.5 16.0 %collective-permute-done.67 = bf16[2,4,2,32,1024]{4,3,2,1,0:T(8,128)(2,1)S(1)} collective-permute-done((bf16[2,4,2,32,1024]{4,3,2,1,0:T(8,128)(2,1)}, bf16[2,4,2,32,1024]{4,3,2,1,0:T(8,128)(2,1)S(1)}, u32[]{:S(2)}, u32[]{:S(2)}) %collective-permute-start.67) | collective-permute-done | bytes 1048608 | tf_op jit(solution)/shard_map/ppermute | solution.py:68
  495.5 3.5 collective-permute-done.68
  499.0 6.3 %collective-permute-done.66 = bf16[4,2,32,1024]{3,2,1,0:T(8,128)(2,1)S(1)} collective-permute-done((bf16[4,2,32,1024]{3,2,1,0:T(8,128)(2,1)S(1)}, bf16[4,2,32,1024]{3,2,1,0:T(8,128)(2,1)S(1)}, u32[]{:S(2)}, u32[]{:S(2)}) %collective-permute-start.66) | collective-permute-done | bytes 524320 | tf_op jit(solution)/shard_map/ppermute | solution.py:68
  510.5 3.3 collective-permute-start.79
  518.2 3.3 collective-permute-done.70
  529.7 15.3 %collective-permute-start.81 = (bf16[4,32,1024]{2,1,0:T(8,128)(2,1)S(1)}, bf16[4,32,1024]{2,1,0:T(8,128)(2,1)S(1)}, u32[]{:S(2)}, u32[]{:S(2)}) collective-permute-start(bf16[4,32,1024]{2,1,0:T(8,128)(2,1)S(1)} %fusion.13), channel_id=1, source_target_pairs={{0,128},{1,129},{2,130},{3,131},{32,160},{33,161},{34,162},{35,163... | collective-permute-start | bytes 786440 | tf_op jit(solution)/shard_map/ppermute | solution.py:68
  545.0 78.1 %all_gather.11 = f32[32,8,128]{2,1,0:T(8,128)S(1)} all-gather(f32[1,8,128]{2,1,0:T(8,128)S(1)} %bitcast.206), channel_id=1, replica_groups=mesh['dp'=8,'section'=8,'fsdp'=4] {'dp','fsdp'}, dimensions={0}, use_global_device_ids=true | all-gather | bytes 135168 | tf_op jit(solution)/shard_map/all_gather | solution.py:595
  (492 shorter events, 182.8 us)
Async XLA Ops:
  32.5 112.7 %collective-permute-start.10 = (bf16[8,2,32,1024]{3,2,1,0:T(8,128)(2,1)}, bf16[8,2,32,1024]{3,2,1,0:T(8,128)(2,1)}, u32[]{:S(2)}, u32[]{:S(2)}) collective-permute-start(bf16[8,2,32,1024]{3,2,1,0:T(8,128)(2,1)} %tie.9.refs_1_), channel_id=1, source_target_pairs={{0,1},{1,2},{2,3},{3,0},{32,33},{33,34},{34,35},{35,32},{64,65},{6... | collective-permute-start | bytes 3145736 | tf_op jit(solution)/shard_map/ppermute | solution.py:68
  34.1 112.7 %collective-permute-start.9 = (bf16[8,2,32,1024]{3,2,1,0:T(8,128)(2,1)}, bf16[8,2,32,1024]{3,2,1,0:T(8,128)(2,1)}, u32[]{:S(2)}, u32[]{:S(2)}) collective-permute-start(bf16[8,2,32,1024]{3,2,1,0:T(8,128)(2,1)} %tie.9.refs_1_), channel_id=1, source_target_pairs={{0,3},{1,0},{2,1},{3,2},{32,35},{33,32},{34,33},{35,34},{64,67},{6... | collective-permute-start | bytes 3145736 | tf_op jit(solution)/shard_map/ppermute | solution.py:68
  35.8 28.3 %collective-permute-start.17 = (bf16[2,128,1024]{2,1,0:T(8,128)(2,1)S(1)}, bf16[2,128,1024]{2,1,0:T(8,128)(2,1)}, u32[]{:S(2)}, u32[]{:S(2)}) collective-permute-start(bf16[2,128,1024]{2,1,0:T(8,128)(2,1)S(1)} %bitcast.203), channel_id=1, source_target_pairs={{0,1},{1,2},{2,3},{3,32},{32,33},{33,34},{34,35},{35,64},{64,65},{... | collective-permute-start | bytes 1572872 | tf_op jit(solution)/shard_map/ppermute | solution.py:37
  38.0 106.5 %collective-permute-start.19 = (bf16[2,128,1024]{2,1,0:T(8,128)(2,1)S(1)}, bf16[2,128,1024]{2,1,0:T(8,128)(2,1)}, u32[]{:S(2)}, u32[]{:S(2)}) collective-permute-start(bf16[2,128,1024]{2,1,0:T(8,128)(2,1)S(1)} %bitcast.204), channel_id=1, source_target_pairs={{1,0},{2,1},{3,2},{32,3},{33,32},{34,33},{35,34},{64,35},{65,64},{... | collective-permute-start | bytes 1572872 | tf_op jit(solution)/shard_map/ppermute | solution.py:37
  45.9 109.0 %collective-permute-start.14 = (bf16[8,2,32,1024]{3,2,1,0:T(8,128)(2,1)S(1)}, bf16[8,2,32,1024]{3,2,1,0:T(8,128)(2,1)}, u32[]{:S(2)}, u32[]{:S(2)}) collective-permute-start(bf16[8,2,32,1024]{3,2,1,0:T(8,128)(2,1)S(1)} %copy-done.108), channel_id=1, source_target_pairs={{0,32},{1,33},{2,34},{3,35},{32,64},{33,65},{34,66},{35,67},{64,96... | collective-permute-start | bytes 3145736 | tf_op jit(solution)/shard_map/ppermute | solution.py:68
  64.2 100.8 %collective-permute-start.13 = (bf16[8,2,32,1024]{3,2,1,0:T(8,128)(2,1)S(1)}, bf16[8,2,32,1024]{3,2,1,0:T(8,128)(2,1)}, u32[]{:S(2)}, u32[]{:S(2)}) collective-permute-start(bf16[8,2,32,1024]{3,2,1,0:T(8,128)(2,1)S(1)} %copy-done.108), channel_id=1, source_target_pairs={{0,96},{1,97},{2,98},{3,99},{32,0},{33,1},{34,2},{35,3},{64,32},{6... | collective-permute-start | bytes 3145736 | tf_op jit(solution)/shard_map/ppermute | solution.py:68
  144.5 21.7 %collective-permute-start.22 = (bf16[2,128,1024]{2,1,0:T(8,128)(2,1)}, bf16[2,128,1024]{2,1,0:T(8,128)(2,1)S(1)}, u32[]{:S(2)}, u32[]{:S(2)}) collective-permute-start(bf16[2,128,1024]{2,1,0:T(8,128)(2,1)} %param.8), channel_id=1, source_target_pairs={{22,28},{23,29},{52,30},{53,31},{54,60},{55,61},{84,62},{85,63},{8... | collective-permute-start | bytes 1572872 | tf_op jit(solution)/shard_map/ppermute | solution.py:48
  145.2 24.3 %collective-permute-start.21 = (bf16[2,128,1024]{2,1,0:T(8,128)(2,1)}, bf16[2,128,1024]{2,1,0:T(8,128)(2,1)}, u32[]{:S(2)}, u32[]{:S(2)}) collective-permute-start(bf16[2,128,1024]{2,1,0:T(8,128)(2,1)} %param.8), channel_id=1, source_target_pairs={{21,28},{22,29},{23,30},{52,31},{53,60},{54,61},{55,62},{84,63},{8... | collective-permute-start | bytes 1572872 | tf_op jit(solution)/shard_map/ppermute | solution.py:48
  146.7 22.8 %collective-permute-start.18 = (bf16[2,128,1024]{2,1,0:T(8,128)(2,1)}, bf16[2,128,1024]{2,1,0:T(8,128)(2,1)}, u32[]{:S(2)}, u32[]{:S(2)}) collective-permute-start(bf16[2,128,1024]{2,1,0:T(8,128)(2,1)} %collective-permute-done.17.refs_12_), channel_id=1, source_target_pairs={{0,1},{1,2},{2,3},{3,32},{32,33},{33,34},{34,35},{35,64},{64,65},{... | collective-permute-start | bytes 1572872 | tf_op jit(solution)/shard_map/ppermute | solution.py:37
  154.9 19.9 %collective-permute-start.20 = (bf16[2,128,1024]{2,1,0:T(8,128)(2,1)}, bf16[2,128,1024]{2,1,0:T(8,128)(2,1)}, u32[]{:S(2)}, u32[]{:S(2)}) collective-permute-start(bf16[2,128,1024]{2,1,0:T(8,128)(2,1)} %collective-permute-done.19.refs_14_), channel_id=1, source_target_pairs={{1,0},{2,1},{3,2},{32,3},{33,32},{34,33},{35,34},{64,35},{65,64},{... | collective-permute-start | bytes 1572872 | tf_op jit(solution)/shard_map/ppermute | solution.py:37
  306.1 108.9 %collective-permute-start.41 = (bf16[128,1024]{1,0:T(8,128)(2,1)S(1)}, bf16[128,1024]{1,0:T(8,128)(2,1)S(1)}, u32[]{:S(2)}, u32[]{:S(2)}) collective-permute-start(bf16[128,1024]{1,0:T(8,128)(2,1)S(1)} %get-tuple-element.147.refs_16_), channel_id=1, source_target_pairs={{4,0},{5,1},{6,2},{7,3},{36,32},{37,33},{38,34},{39,35},{68,64},{6... | collective-permute-start | bytes 786440 | tf_op jit(solution)/shard_map/ppermute | solution.py:48
  307.4 117.7 %collective-permute-start.42 = (bf16[128,1024]{1,0:T(8,128)(2,1)S(1)}, bf16[128,1024]{1,0:T(8,128)(2,1)S(1)}, u32[]{:S(2)}, u32[]{:S(2)}) collective-permute-start(bf16[128,1024]{1,0:T(8,128)(2,1)S(1)} %get-tuple-element.147.refs_16_), channel_id=1, source_target_pairs={{5,0},{6,1},{7,2},{36,3},{37,32},{38,33},{39,34},{68,35},{69,64},{... | collective-permute-start | bytes 786440 | tf_op jit(solution)/shard_map/ppermute | solution.py:48
  308.7 116.4 %collective-permute-start.43 = (bf16[128,1024]{1,0:T(8,128)(2,1)S(1)}, bf16[128,1024]{1,0:T(8,128)(2,1)S(1)}, u32[]{:S(2)}, u32[]{:S(2)}) collective-permute-start(bf16[128,1024]{1,0:T(8,128)(2,1)S(1)} %get-tuple-element.147.refs_16_), channel_id=1, source_target_pairs={{6,0},{7,1},{36,2},{37,3},{38,32},{39,33},{68,34},{69,35},{70,64},... | collective-permute-start | bytes 786440 | tf_op jit(solution)/shard_map/ppermute | solution.py:48
  425.9 15.6 %collective-permute-start.62 = (bf16[128,1024]{1,0:T(8,128)(2,1)}, bf16[128,1024]{1,0:T(8,128)(2,1)S(1)}, u32[]{:S(2)}, u32[]{:S(2)}) collective-permute-start(bf16[128,1024]{1,0:T(8,128)(2,1)} %tie.17.refs_22_), channel_id=1, source_target_pairs={{4,0},{5,1},{6,2},{7,3},{36,32},{37,33},{38,34},{39,35},{68,64},{6... | collective-permute-start | bytes 786440 | tf_op jit(solution)/shard_map/ppermute | solution.py:48
  427.1 16.9 %collective-permute-start.63 = (bf16[128,1024]{1,0:T(8,128)(2,1)}, bf16[128,1024]{1,0:T(8,128)(2,1)S(1)}, u32[]{:S(2)}, u32[]{:S(2)}) collective-permute-start(bf16[128,1024]{1,0:T(8,128)(2,1)} %tie.17.refs_22_), channel_id=1, source_target_pairs={{5,0},{6,1},{7,2},{36,3},{37,32},{38,33},{39,34},{68,35},{69,64},{... | collective-permute-start | bytes 786440 | tf_op jit(solution)/shard_map/ppermute | solution.py:48
  428.4 15.6 %collective-permute-start.64 = (bf16[128,1024]{1,0:T(8,128)(2,1)}, bf16[128,1024]{1,0:T(8,128)(2,1)S(1)}, u32[]{:S(2)}, u32[]{:S(2)}) collective-permute-start(bf16[128,1024]{1,0:T(8,128)(2,1)} %tie.17.refs_22_), channel_id=1, source_target_pairs={{6,0},{7,1},{36,2},{37,3},{38,32},{39,33},{68,34},{69,35},{70,64},... | collective-permute-start | bytes 786440 | tf_op jit(solution)/shard_map/ppermute | solution.py:48
  466.0 21.6 %collective-permute-start.67 = (bf16[2,4,2,32,1024]{4,3,2,1,0:T(8,128)(2,1)}, bf16[2,4,2,32,1024]{4,3,2,1,0:T(8,128)(2,1)S(1)}, u32[]{:S(2)}, u32[]{:S(2)}) collective-permute-start(bf16[2,4,2,32,1024]{4,3,2,1,0:T(8,128)(2,1)} %get-tuple-element.241), channel_id=1, source_target_pairs={{0,3},{1,0},{2,1},{3,2},{32,35},{33,32},{34,33},{35,34},{64,67},{6... | collective-permute-start | bytes 3145736 | tf_op jit(solution)/shard_map/ppermute | solution.py:68
  467.1 23.5 %collective-permute-start.65 = (bf16[2,4,2,32,1024]{4,3,2,1,0:T(8,128)(2,1)}, bf16[2,4,2,32,1024]{4,3,2,1,0:T(8,128)(2,1)}, u32[]{:S(2)}, u32[]{:S(2)}) collective-permute-start(bf16[2,4,2,32,1024]{4,3,2,1,0:T(8,128)(2,1)} %get-tuple-element.240), channel_id=1, source_target_pairs={{0,1},{1,2},{2,3},{3,0},{32,33},{33,34},{34,35},{35,32},{64,65},{6... | collective-permute-start | bytes 3145736 | tf_op jit(solution)/shard_map/ppermute | solution.py:68
  469.5 23.4 %collective-permute-start.75 = (bf16[2,4,2,32,1024]{4,3,2,1,0:T(8,128)(2,1)}, bf16[2,4,2,32,1024]{4,3,2,1,0:T(8,128)(2,1)S(1)}, u32[]{:S(2)}, u32[]{:S(2)}) collective-permute-start(bf16[2,4,2,32,1024]{4,3,2,1,0:T(8,128)(2,1)} %get-tuple-element.246), channel_id=1, source_target_pairs={{0,96},{1,97},{2,98},{3,99},{32,0},{33,1},{34,2},{35,3},{64,32},{6... | collective-permute-start | bytes 3145736 | tf_op jit(solution)/shard_map/ppermute | solution.py:68
  469.5 23.7 %collective-permute-start.73 = (bf16[2,4,2,32,1024]{4,3,2,1,0:T(8,128)(2,1)}, bf16[2,4,2,32,1024]{4,3,2,1,0:T(8,128)(2,1)S(1)}, u32[]{:S(2)}, u32[]{:S(2)}) collective-permute-start(bf16[2,4,2,32,1024]{4,3,2,1,0:T(8,128)(2,1)} %get-tuple-element.245), channel_id=1, source_target_pairs={{0,32},{1,33},{2,34},{3,35},{32,64},{33,65},{34,66},{35,67},{64,96... | collective-permute-start | bytes 3145736 | tf_op jit(solution)/shard_map/ppermute | solution.py:68
  492.0 13.3 %collective-permute-start.66 = (bf16[4,2,32,1024]{3,2,1,0:T(8,128)(2,1)S(1)}, bf16[4,2,32,1024]{3,2,1,0:T(8,128)(2,1)S(1)}, u32[]{:S(2)}, u32[]{:S(2)}) collective-permute-start(bf16[4,2,32,1024]{3,2,1,0:T(8,128)(2,1)S(1)} %fusion.4), channel_id=1, source_target_pairs={{0,1},{1,2},{2,3},{3,0},{32,33},{33,34},{34,35},{35,32},{64,65},{6... | collective-permute-start | bytes 1572872 | tf_op jit(solution)/shard_map/ppermute | solution.py:68
  493.1 16.5 %collective-permute-start.76 = (bf16[4,2,32,1024]{3,2,1,0:T(8,128)(2,1)S(1)}, bf16[4,2,32,1024]{3,2,1,0:T(8,128)(2,1)S(1)}, u32[]{:S(2)}, u32[]{:S(2)}) collective-permute-start(bf16[4,2,32,1024]{3,2,1,0:T(8,128)(2,1)S(1)} %fusion.7), channel_id=1, source_target_pairs={{0,96},{1,97},{2,98},{3,99},{32,0},{33,1},{34,2},{35,3},{64,32},{6... | collective-permute-start | bytes 1572872 | tf_op jit(solution)/shard_map/ppermute | solution.py:68
  493.4 16.2 %collective-permute-start.74 = (bf16[4,2,32,1024]{3,2,1,0:T(8,128)(2,1)S(1)}, bf16[4,2,32,1024]{3,2,1,0:T(8,128)(2,1)S(1)}, u32[]{:S(2)}, u32[]{:S(2)}) collective-permute-start(bf16[4,2,32,1024]{3,2,1,0:T(8,128)(2,1)S(1)} %fusion.6), channel_id=1, source_target_pairs={{0,32},{1,33},{2,34},{3,35},{32,64},{33,65},{34,66},{35,67},{64,96... | collective-permute-start | bytes 1572872 | tf_op jit(solution)/shard_map/ppermute | solution.py:68
  529.7 94.0 %collective-permute-start.81 = (bf16[4,32,1024]{2,1,0:T(8,128)(2,1)S(1)}, bf16[4,32,1024]{2,1,0:T(8,128)(2,1)S(1)}, u32[]{:S(2)}, u32[]{:S(2)}) collective-permute-start(bf16[4,32,1024]{2,1,0:T(8,128)(2,1)S(1)} %fusion.13), channel_id=1, source_target_pairs={{0,128},{1,129},{2,130},{3,131},{32,160},{33,161},{34,162},{35,163... | collective-permute-start | bytes 786440 | tf_op jit(solution)/shard_map/ppermute | solution.py:68
  (188 other events, 708.2 us)
